TPU v7x, 128 devices: a whole 4x4x4 slice. The times are simulated.
128 devices in a mesh: seq: 32 (over z, y_lo, x), tp: 4 (over y_hi, core).
Axes of the slice: x: 4, y: 4 (y_hi: 2, y_lo: 2; y = y_hi * 2 + y_lo), z: 4, core: 2. Of those that a mesh axis runs over, the one named last changes fastest.
Arguments:
- tokens: bfloat16 [16384, 4096], P(('seq', 'tp')), may hold values from -64 to 64, as said below
- joined_projection_weight: bfloat16 [4096, 6144], P(None, 'tp'), may hold values from -0.09375 to 0.09375
- adapter_down_weight: bfloat16 [4096, 64], replicated, may hold values from -0.09375 to 0.09375
- adapter_up_weight: bfloat16 [64, 6144], P(None, 'tp'), may hold values from -0.75 to 0.75
- document_index: int32 [16384], replicated, may hold values from 0 to 3, as said below
- query_to_key_head: int32 [32], replicated, may hold values from 0 to 7, as said below
Outputs:
- context: bfloat16 [16384, 4096], P(('seq', 'tp'))
Inputs may be any that keep to these rules, and one draw needn't show every extreme that they name: `tokens`: rows of order one, except in the hidden draw where some rows have larger scales. `query_to_key_head`: each of 0 to 7 is named by exactly 4 query heads. `document_index`: never falling, starting at 0; each of the 4 documents covers 16384 / 16 or more positions.
All inputs are finite; a program needn't handle non-finite values.
Results may differ from a plain program's by a relative error of at most 0.012.
The roundings to bfloat16 on the way count: a program that leaves them out, or rounds other values in their place, can miss the bound.
Values may be sent and summed in bfloat16 or wider, within the bound.
No kernel may reach another device: no remote copies, remote signals or barrier semaphores. Data moves between devices by JAX's collectives and lax.ppermute only.
A program may use at most 128 MiB of HBM per device.

v0:
```python
import jax
import jax.numpy as jnp
from jax import lax
from jax.sharding import PartitionSpec as P

H = 32
KV = 8
DH = 128


ADAPTER_SCALE = 0.5
THETA = 500000.0
NEG_BIG = -1e30


def side_by_side(arrays, axis, dim, along):
    both = jnp.concatenate(arrays, axis=along)
    whole, at, outs = (lax.all_gather(both, axis, axis=dim, tiled=True), 0, [])
    for a in arrays:
        outs.append(lax.slice_in_dim(whole, at, at + a.shape[along], axis=along))
        at += a.shape[along]
    return tuple(outs)


def rotate(values, places):
    half_dim = values.shape[-1] // 2
    frequency = THETA ** (-(jnp.arange(half_dim, dtype=jnp.float32) * 2.0) / values.shape[-1])
    angles = places[:, None] * frequency[None, :]
    cosine = jnp.cos(angles)[:, None, :]
    sine_part = jnp.sin(angles)[:, None, :]
    front_half = values[..., :half_dim]
    back_half = values[..., half_dim:]
    return jnp.concatenate(
        [front_half * cosine - back_half * sine_part, back_half * cosine + front_half * sine_part],
        axis=-1,
    )


def expand_heads(grouped, query_to_key_head):
    groups = grouped.shape[1]
    select = (query_to_key_head[None, :] == jnp.arange(groups, dtype=jnp.int32)[:, None]).astype(
        jnp.bfloat16
    )
    return jnp.einsum("tgd,gh->thd", grouped, select, preferred_element_type=jnp.float32).astype(
        jnp.bfloat16
    )


def per_device(
    tokens,
    joined_projection_weight,
    adapter_down_weight,
    adapter_up_weight,
    document_index,
    query_to_key_head,
):
    tp_count = lax.axis_size("tp")
    seq_count = lax.axis_size("seq")
    tp_rank = lax.axis_index("tp")
    seq_rank = lax.axis_index("seq")
    own_rows = tokens.shape[0]
    head_dim = DH
    query_local = H // tp_count
    kv_local = KV // tp_count
    shrunk = jnp.dot(tokens, adapter_down_weight, preferred_element_type=jnp.float32).astype(
        jnp.bfloat16
    )
    collected_rows, reduced_token_rows = (
        lax.all_gather(tokens, "tp", axis=0, tiled=True),
        lax.all_gather(shrunk, "tp", axis=0, tiled=True),
    )
    joined_output = jnp.dot(
        collected_rows, joined_projection_weight, preferred_element_type=jnp.float32
    )
    joined_output = joined_output + ADAPTER_SCALE * jnp.dot(
        reduced_token_rows, adapter_up_weight, preferred_element_type=jnp.float32
    )
    block_rows = collected_rows.shape[0]
    places = (seq_rank * block_rows + jnp.arange(block_rows, dtype=jnp.int32)).astype(jnp.float32)
    key_start_col = query_local * head_dim
    value_start_col = (query_local + kv_local) * head_dim
    queries = rotate(
        joined_output[:, :key_start_col].reshape(block_rows, query_local, head_dim), places
    ).astype(jnp.bfloat16)
    keys = rotate(
        joined_output[:, key_start_col:value_start_col].reshape(block_rows, kv_local, head_dim),
        places,
    ).astype(jnp.bfloat16)
    values_local = (
        joined_output[:, value_start_col:]
        .reshape(block_rows, kv_local, head_dim)
        .astype(jnp.bfloat16)
    )
    query_heads, key_group, value_group = (
        lax.all_to_all(queries, "tp", split_axis=0, concat_axis=1, tiled=True),
        lax.all_to_all(keys, "tp", split_axis=0, concat_axis=1, tiled=True),
        lax.all_to_all(values_local, "tp", split_axis=0, concat_axis=1, tiled=True),
    )
    key_heads = expand_heads(key_group, query_to_key_head)
    value_heads = expand_heads(value_group, query_to_key_head)
    query_shard, key_part, value_part = (
        lax.all_to_all(query_heads, "seq", split_axis=1, concat_axis=0, tiled=True),
        lax.all_to_all(key_heads, "seq", split_axis=1, concat_axis=0, tiled=True),
        lax.all_to_all(value_heads, "seq", split_axis=1, concat_axis=0, tiled=True),
    )
    heads_part = key_part.shape[1]
    key_blocks = key_part.reshape(seq_count, 1, own_rows, heads_part, head_dim)
    value_blocks = value_part.reshape(seq_count, 1, own_rows, heads_part, head_dim)
    key_whole, value_whole = side_by_side((key_blocks, value_blocks), "tp", 1, 0)
    key_shard = key_whole.reshape(-1, heads_part, head_dim)
    value_shard = value_whole.reshape(-1, heads_part, head_dim)
    query_count = query_shard.shape[0]
    heads_here = query_shard.shape[1]
    query_block = min(1024, query_count)
    key_block = 2 * query_block
    per_block = query_block * tp_count // key_block
    local_index = jnp.arange(query_count, dtype=jnp.int32)
    query_places = (
        local_index // own_rows * block_rows + tp_rank * own_rows + local_index % own_rows
    )
    query_segments = jnp.take(document_index, query_places)
    scale = head_dim ** (-0.5)

    def attend_block(block_index):
        start = block_index * query_block
        query_tile = lax.dynamic_slice_in_dim(query_shard, start, query_block, 0)
        tile_places = lax.dynamic_slice_in_dim(query_places, start, query_block, 0)
        tile_segments = lax.dynamic_slice_in_dim(query_segments, start, query_block, 0)

        def key_step(key_index, carry):
            running_max, running_sum, accumulated = carry
            key_start = key_index * key_block
            key_tile = lax.dynamic_slice_in_dim(key_shard, key_start, key_block, 0)
            value_tile = lax.dynamic_slice_in_dim(value_shard, key_start, key_block, 0)
            key_places = key_start + jnp.arange(key_block, dtype=jnp.int32)
            key_segments = lax.dynamic_slice_in_dim(document_index, key_start, key_block, 0)
            scores = (
                jnp.einsum("qhd,khd->qhk", query_tile, key_tile, preferred_element_type=jnp.float32)
                * scale
            )
            allowed = (key_places[None, :] <= tile_places[:, None]) & (
                key_segments[None, :] == tile_segments[:, None]
            )
            scores = jnp.where(allowed[:, None, :], scores, -jnp.inf)
            new_max = jnp.maximum(running_max, jnp.max(scores, axis=-1))
            factor = jnp.exp(running_max - new_max)
            powers = jnp.exp(scores - new_max[..., None])
            running_sum = running_sum * factor + jnp.sum(powers, axis=-1)
            update = jnp.einsum(
                "qhk,khd->qhd",
                powers.astype(jnp.bfloat16),
                value_tile,
                preferred_element_type=jnp.float32,
            )
            accumulated = accumulated * factor[..., None] + update
            return (new_max, running_sum, accumulated)

        initial = (
            jnp.full((query_block, heads_here), NEG_BIG, jnp.float32),
            jnp.zeros((query_block, heads_here), jnp.float32),
            jnp.zeros((query_block, heads_here, head_dim), jnp.float32),
        )
        final_max, final_sum, accumulated = lax.fori_loop(
            0, (block_index + 1) * per_block, key_step, initial
        )
        return (accumulated / final_sum[..., None]).astype(jnp.bfloat16)

    tiles = lax.map(attend_block, jnp.arange(query_count // query_block, dtype=jnp.int32))
    context_heads = tiles.reshape(query_count, heads_here, head_dim)
    context_rows = lax.all_to_all(context_heads, "seq", split_axis=0, concat_axis=1, tiled=True)
    return context_rows.reshape(own_rows, -1)


def solution(mesh):
    return jax.shard_map(
        per_device,
        mesh=mesh,
        in_specs=(P(("seq", "tp"), None), P(None, "tp"), P(), P(None, "tp"), P(), P()),
        out_specs=P(("seq", "tp"), None),
        check_vma=False,
    )
```

profile of v0, /device:TPU:0, one launch (start us, length us, event | category | flops | bytes accessed | tf_op | source)
XLA Modules:
  0.0 425.9 jit_solution(5476492631415542965)
XLA Ops:
  9.3 6.8 %all_gather.10 = bf16[512,64]{0,1:T(8,128)(2,1)S(1)} all-gather(bf16[128,64]{0,1:T(8,128)(2,1)S(1)} %convolution_convert_fusion.2), channel_id=1, replica_groups=mesh['seq'=32,'tp'=4] {'tp'}, dimensions={0}, use_global_device_ids=true | all-gather | bytes 81920 | tf_op jit(solution)/shard_map/all_gather | solution.py:70
  17.1 33.0 %all-gather.3.cloned.1.call-done = bf16[512,4096]{1,0:T(8,128)(2,1)} async-done(((bf16[128,4096]{1,0:T(8,128)(2,1)}), bf16[512,4096]{1,0:T(8,128)(2,1)}) %all-gather.3.cloned.1.call-update) | async-done | bytes 4194320 | tf_op jit(solution)/shard_map/all_gather | solution.py:69
  50.1 10.5 %fusion.43 = f32[512,1536]{1,0:T(8,128)S(1)} fusion(bf16[512,4096]{1,0:T(8,128)(2,1)} %all-gather.3.cloned.1.call-done, bf16[4096,1536]{1,0:T(8,128)(2,1)} %param.11), kind=kOutput, calls=%fused_computation.76 | convolution fusion | flops 6442450944 | bytes 19922944 | tf_op jit(solution)/shard_map/dot_general | solution.py:72
  70.7 5.7 %all-to-all-done.2 = bf16[512,2,128]{2,1,0:T(2,128)(2,1)S(1)} async-done(((bf16[512,2,128]{2,1,0:T(2,128)(2,1)}), bf16[512,2,128]{2,1,0:T(2,128)(2,1)S(1)}, u32[]{:S(2)}, u32[]{:S(2)}) %all-to-all-start.2) | async-done | bytes 262176 | tf_op jit(solution)/shard_map/all_to_all | solution.py:96
  81.8 5.4 %all-to-all-done.4 = bf16[512,2,128]{2,1,0:T(2,128)(2,1)S(1)} async-done(((bf16[512,2,128]{2,1,0:T(2,128)(2,1)}), bf16[512,2,128]{2,1,0:T(2,128)(2,1)S(1)}, u32[]{:S(2)}, u32[]{:S(2)}) %all-to-all-start.4) | async-done | bytes 262176 | tf_op jit(solution)/shard_map/all_to_all | solution.py:97
  87.2 7.3 %all-to-all-start.3 = ((bf16[128,32,128]{2,0,1:T(8,128)(2,1)}), bf16[128,32,128]{2,0,1:T(8,128)(2,1)S(1)}, u32[]{:S(2)}, u32[]{:S(2)}) async-start(bf16[128,32,128]{2,0,1:T(8,128)(2,1)} %copy.26), calls=%async_computation.3 | async-start | bytes 2097152 | tf_op jit(solution)/shard_map/all_to_all | solution.py:103
  95.6 15.3 %all-to-all-done.3 = bf16[128,32,128]{2,0,1:T(8,128)(2,1)S(1)} async-done(((bf16[128,32,128]{2,0,1:T(8,128)(2,1)}), bf16[128,32,128]{2,0,1:T(8,128)(2,1)S(1)}, u32[]{:S(2)}, u32[]{:S(2)}) %all-to-all-start.3) | async-done | bytes 1048608 | tf_op jit(solution)/shard_map/all_to_all | solution.py:103
  111.0 21.0 %all_to_all.117 = bf16[128,32,128]{2,0,1:T(8,128)(2,1)S(1)} all-to-all(bf16[128,32,128]{2,0,1:T(8,128)(2,1)S(1)} %copy.28), channel_id=1, replica_groups=mesh['seq'=32,'tp'=4] {'seq'}, dimensions={1} | all-to-all | bytes 2097152 | tf_op jit(solution)/shard_map/all_to_all | solution.py:104
  141.8 27.1 %all-to-all-done = bf16[512,8,128]{2,1,0:T(8,128)(2,1)S(1)} async-done(((bf16[512,8,128]{2,1,0:T(8,128)(2,1)}), bf16[512,8,128]{2,1,0:T(8,128)(2,1)S(1)}, u32[]{:S(2)}, u32[]{:S(2)}) %all-to-all-start) | async-done | bytes 1048608 | tf_op jit(solution)/shard_map/all_to_all | solution.py:95
  170.1 4.5 %all-to-all-start.1 = ((bf16[128,32,128]{2,0,1:T(8,128)(2,1)}), bf16[128,32,128]{2,0,1:T(8,128)(2,1)S(1)}, u32[]{:S(2)}, u32[]{:S(2)}) async-start(bf16[128,32,128]{2,0,1:T(8,128)(2,1)} %bitcast.18), calls=%async_computation.1 | async-start | bytes 2097152 | tf_op jit(solution)/shard_map/all_to_all | solution.py:102
  174.7 23.0 %gather_fusion = s32[4096]{0:T(1024)S(1)} fusion(s32[16384]{0:T(1024)S(1)} %copy-done.2, s32[4096]{0:T(1024)S(1)} %broadcast_clamp_fusion), kind=kCustom, calls=%fused_computation | custom fusion | bytes 49152 | tf_op jit(solution)/shard_map/jit(_take)/gather | solution.py:121
  197.7 17.3 %all-gather.5.cloned.1.call-done = bf16[64,4,128,1,128]{4,2,3,0,1:T(8,128)(2,1)} async-done(((bf16[64,1,128,1,128]{4,2,3,0,1:T(8,128)(2,1)}), bf16[64,4,128,1,128]{4,2,3,0,1:T(8,128)(2,1)}) %all-gather.5.cloned.1.call-update) | async-done | bytes 8388624 | tf_op jit(solution)/shard_map/all_gather | solution.py:18
  215.1 3.8 fusion.42
  223.4 162.6 %while.25 = (s32[]{:T(128)}, bf16[4,1024,1,128]{3,1,0,2:T(8,128)(2,1)S(1)}, s32[4]{0:T(128)S(1)}, bf16[4096,1,128]{2,0,1:T(8,128)(2,1)S(1)}, s32[4096]{0:T(1024)...) while((s32[]{:T(128)}, ...), condition=%wide.region_5.6_spmd, body=%wide.region_0.0_spmd.sunk | while | flops 1095241728 | bytes 30552712 | solution.py:168
  225.5 15.3 %while.26 = (s32[]{:T(128)}, f32[1024,1]{0,1:T(1,128)S(1)}, f32[1024,1]{0,1:T(1,128)S(1)}, f32[1024,1,128]{0,2,1:T(8,128)S(1)}, s32[]{:T(128)}, /*index=5*/s32[1...) while((s32[]{:T(128)}, f32[1024,1]{0,1:T(1,128)S(1)}, ...), condition=%wide.region_4.4_spmd, body=%wide.region_1.3_spmd.sunk | while | flops 1094979584 | bytes 27640012 | solution.py:163
  225.5 3.7 fusion.61
  243.1 30.7 %while.26 = (s32[]{:T(128)}, f32[1024,1]{0,1:T(1,128)S(1)}, f32[1024,1]{0,1:T(1,128)S(1)}, f32[1024,1,128]{0,2,1:T(8,128)S(1)}, s32[]{:T(128)}, /*index=5*/s32[1...) while((s32[]{:T(128)}, f32[1024,1]{0,1:T(1,128)S(1)}, ...), condition=%wide.region_4.4_spmd, body=%wide.region_1.3_spmd.sunk | while | flops 1094979584 | bytes 27640012 | solution.py:163
  243.2 3.7 fusion.61
  276.1 46.0 %while.26 = (s32[]{:T(128)}, f32[1024,1]{0,1:T(1,128)S(1)}, f32[1024,1]{0,1:T(1,128)S(1)}, f32[1024,1,128]{0,2,1:T(8,128)S(1)}, s32[]{:T(128)}, /*index=5*/s32[1...) while((s32[]{:T(128)}, f32[1024,1]{0,1:T(1,128)S(1)}, ...), condition=%wide.region_4.4_spmd, body=%wide.region_1.3_spmd.sunk | while | flops 1094979584 | bytes 27640012 | solution.py:163
  276.2 3.7 fusion.61
  324.4 61.3 %while.26 = (s32[]{:T(128)}, f32[1024,1]{0,1:T(1,128)S(1)}, f32[1024,1]{0,1:T(1,128)S(1)}, f32[1024,1,128]{0,2,1:T(8,128)S(1)}, s32[]{:T(128)}, /*index=5*/s32[1...) while((s32[]{:T(128)}, f32[1024,1]{0,1:T(1,128)S(1)}, ...), condition=%wide.region_4.4_spmd, body=%wide.region_1.3_spmd.sunk | while | flops 1094979584 | bytes 27640012 | solution.py:163
  324.5 3.7 fusion.61
  388.3 22.4 %all_to_all.118 = bf16[32,2,8192]{2,1,0:T(2,128)(2,1)} all-to-all(bf16[32,2,8192]{2,1,0:T(2,128)(2,1)S(1)} %reshape.296), channel_id=1, replica_groups=mesh['seq'=32,'tp'=4] {'seq'}, dimensions={0} | all-to-all | bytes 2097152 | tf_op jit(solution)/shard_map/all_to_all | solution.py:170
  410.7 4.4 %reshape.297 = bf16[4096,1,128]{2,1,0:T(2,128)(2,1)S(1)} reshape(bf16[32,2,8192]{2,1,0:T(2,128)(2,1)} %all_to_all.118) | data formatting | bytes 2097152
  (252 shorter events, 183.2 us)
Async XLA Ops:
  6.5 1.0 copy-start
  6.5 43.5 %all-gather.3.cloned.1.call-start = ((), (), s32[]{:S(2)}) async-start(), calls=%async_computation.7 | async-start | bytes 5242880 | tf_op jit(solution)/shard_map/all_gather | solution.py:69
  17.1 43.5 %copy-start.4 = (bf16[64,1536]{1,0:T(8,128)(2,1)S(1)}, bf16[64,1536]{1,0:T(8,128)(2,1)}, u32[]{:S(2)}) copy-start(bf16[64,1536]{1,0:T(8,128)(2,1)} %param.13) | copy-start | bytes 589828
  61.2 1.7 copy-start.3
  62.9 17.1 %copy-start.5 = (s32[32]{0:T(128)S(1)}, s32[32]{0:T(128)}, u32[]{:S(2)}) copy-start(s32[32]{0:T(128)} %param.15) | copy-start | bytes 388
  65.4 10.9 %all-to-all-start.2 = ((bf16[512,2,128]{2,1,0:T(2,128)(2,1)}), bf16[512,2,128]{2,1,0:T(2,128)(2,1)S(1)}, u32[]{:S(2)}, u32[]{:S(2)}) async-start(bf16[512,2,128]{2,1,0:T(2,128)(2,1)} %pad_maximum_fusion.1), calls=%async_computation.2 | async-start | bytes 524288 | tf_op jit(solution)/shard_map/all_to_all | solution.py:96
  76.3 10.9 %all-to-all-start.4 = ((bf16[512,2,128]{2,1,0:T(2,128)(2,1)}), bf16[512,2,128]{2,1,0:T(2,128)(2,1)S(1)}, u32[]{:S(2)}, u32[]{:S(2)}) async-start(bf16[512,2,128]{2,1,0:T(2,128)(2,1)} %convert_element_type.40), calls=%async_computation.4 | async-start | bytes 524288 | tf_op jit(solution)/shard_map/all_to_all | solution.py:97
  87.2 23.7 %all-to-all-start.3 = ((bf16[128,32,128]{2,0,1:T(8,128)(2,1)}), bf16[128,32,128]{2,0,1:T(8,128)(2,1)S(1)}, u32[]{:S(2)}, u32[]{:S(2)}) async-start(bf16[128,32,128]{2,0,1:T(8,128)(2,1)} %copy.26), calls=%async_computation.3 | async-start | bytes 2097152 | tf_op jit(solution)/shard_map/all_to_all | solution.py:103
  94.5 120.5 %all-gather.5.cloned.1.call-start = ((), (), s32[]{:S(2)}) async-start(), calls=%async_computation.8 | async-start | bytes 10485760 | tf_op jit(solution)/shard_map/all_gather | solution.py:18
  136.7 38.0 %copy-start.2 = (s32[16384]{0:T(1024)S(1)}, s32[16384]{0:T(1024)}, u32[]{:S(2)}) copy-start(s32[16384]{0:T(1024)} %param.14) | copy-start | bytes 196612
  138.2 30.7 %all-to-all-start = ((bf16[512,8,128]{2,1,0:T(8,128)(2,1)}), bf16[512,8,128]{2,1,0:T(8,128)(2,1)S(1)}, u32[]{:S(2)}, u32[]{:S(2)}) async-start(bf16[512,8,128]{2,1,0:T(8,128)(2,1)} %pad_maximum_fusion), calls=%async_computation | async-start | bytes 2097152 | tf_op jit(solution)/shard_map/all_to_all | solution.py:95
  170.1 53.3 %all-to-all-start.1 = ((bf16[128,32,128]{2,0,1:T(8,128)(2,1)}), bf16[128,32,128]{2,0,1:T(8,128)(2,1)S(1)}, u32[]{:S(2)}, u32[]{:S(2)}) async-start(bf16[128,32,128]{2,0,1:T(8,128)(2,1)} %bitcast.18), calls=%async_computation.1 | async-start | bytes 2097152 | tf_op jit(solution)/shard_map/all_to_all | solution.py:102
  410.7 8.4 %copy-start.1 = (bf16[4096,64]{0,1:T(8,128)(2,1)S(1)}, bf16[4096,64]{0,1:T(8,128)(2,1)}, u32[]{:S(2)}) copy-start(bf16[4096,64]{0,1:T(8,128)(2,1)} %param.12) | copy-start | bytes 1572868
Sparse Core Ops, SparseCore 0:
  9.0 40.9 all-gather.2
  133.7 81.2 all-gather.4
where the time goes:
time: 429 us; the launch traced here: 426 us
  matrix products  141 us (33%)
  waiting for transfers between devices  105 us (24%)
  local copies, waits for them, and re-layouts  54.2 us (13%)
  blocking collectives  50.2 us (12%)
  other arithmetic  33 us (8%)
  starting transfers between devices  22.1 us (5%)
  between operations  13.7 us (3%)
  loops' own time  6.81 us (2%)
    dot_general x20, matrix products, key_step(): jnp.einsum('qhd,khd->qhk', query_tile, key_tile, preferred_element_type=j...  73.8 us
    dot_general x20, matrix products, key_step(): jnp.einsum('qhk,khd->qhd', powers.astype(jnp.bfloat16), value_tile, prefe...  53.8 us
    all_gather x1, waiting for transfers between devices, per_device(): lax.all_gather(tokens, 'tp', axis=0, tiled=True)  33 us
    all_to_all x1, waiting for transfers between devices, per_device(): lax.all_to_all(queries, 'tp', split_axis=0, concat_axis=1, tiled=True)  27.1 us
    reduce_sum x20, other arithmetic, key_step(): running_sum = running_sum * factor + jnp.sum(powers, axis=-1)  23.4 us
    gather x1, local copies, waits for them, and re-layouts, per_device(): query_segments = jnp.take(document_index, query_places)  23 us
    all_to_all x1, blocking collectives, per_device(): lax.all_to_all(context_heads, 'seq', split_axis=0, concat_axis=1, tiled=T...  22.4 us
    all_to_all x1, blocking collectives, per_device(): lax.all_to_all(value_heads, 'seq', split_axis=1, concat_axis=0, tiled=True)  21 us
  transfers between devices with their start and end apart: 7, of which 6 were waited for; matrix products, arithmetic and copies ran while one was open for 11% of the time, Pallas kernels for 0%

commit v1 on v0

v1 whole, which is shorter than its diff:
```python
import functools

import jax
import jax.numpy as jnp
from jax import lax
from jax.experimental import pallas as pl
from jax.experimental.pallas import tpu as pltpu
from jax.sharding import Mesh
from jax.sharding import PartitionSpec as P

H = 32
KV = 8
DH = 128
BLK = 128
THETA = 500000.0
ADAPTER_SCALE = 0.5
NEG_BIG = -1e30
DOCS = 4

NZ, NYL, NX, NYH, NC = 4, 2, 4, 2, 2
ALL = ("z", "yl", "x", "yh", "c")
BF = jnp.bfloat16
F32 = jnp.float32
KEYS = 512


def flat(z, yl, x, yh, c):
    return (((z * NYL + yl) * NX + x) * NYH + yh) * NC + c


def every():
    for z in range(NZ):
        for yl in range(NYL):
            for x in range(NX):
                for yh in range(NYH):
                    for c in range(NC):
                        yield z, yl, x, yh, c


CROSS = [(flat(*d), flat(d[0], 1 - d[1], d[2], 1 - d[3], d[4])) for d in every()]
CROSS_OTHER = [(flat(*d), flat(d[0], 1 - d[1], d[2], 1 - d[3], 1 - d[4])) for d in every()]
SWAP = [(0, 1), (1, 0)]
GROUPS = [
    [flat(z, yl0 ^ yh, (x0 + z) % NX, yh, c) for z in range(NZ) for yh in range(NYH)]
    for x0 in range(NX)
    for yl0 in range(NYL)
    for c in range(NC)
]


def rope_tables(blocks):
    half = DH // 2
    frequency = THETA ** (-(jnp.arange(half, dtype=F32) * 2.0) / DH)
    places = (blocks[:, None] * BLK + jnp.arange(BLK, dtype=jnp.int32)[None, :]).reshape(-1).astype(F32)
    angles = places[:, None] * frequency[None, :]
    cosine, sine = jnp.cos(angles), jnp.sin(angles)
    return jnp.concatenate([cosine, cosine], axis=1), jnp.concatenate([-sine, sine], axis=1)


def rotated(part, cosine, sine):
    return part * cosine + pltpu.roll(part, DH // 2, 1) * sine


def kv_kernel(x0, x1, w, down, up, cosine, sine, out, mid_out, rows, mid):
    step = pl.program_id(0)

    @pl.when(step == 0)
    def _():
        rows[:BLK] = x0[...]
        rows[BLK:] = x1[...]
        mid[...] = jnp.dot(rows[...], down[...], preferred_element_type=F32).astype(BF)
        mid_out[...] = mid[...]

    acc = jnp.dot(rows[...], w[...], preferred_element_type=F32)
    acc = acc + ADAPTER_SCALE * jnp.dot(mid[...], up[...], preferred_element_type=F32)

    @pl.when(step == 0)
    def _():
        for head in range(2):
            part = rotated(acc[:, head * DH:(head + 1) * DH], cosine[...], sine[...]).astype(BF)
            for block in range(2):
                out[block, head, 0] = part[block * BLK:(block + 1) * BLK]

    @pl.when(step == 1)
    def _():
        for head in range(2):
            part = acc[:, head * DH:(head + 1) * DH].astype(BF)
            for block in range(2):
                out[block, head, 0] = part[block * BLK:(block + 1) * BLK]


def q_kernel(x0, x1, mid, w, up, cosine, sine, out, rows):
    step = pl.program_id(0)

    @pl.when(step == 0)
    def _():
        rows[:BLK] = x0[...]
        rows[BLK:] = x1[...]

    acc = jnp.dot(rows[...], w[...], preferred_element_type=F32)
    acc = acc + ADAPTER_SCALE * jnp.dot(mid[...], up[...], preferred_element_type=F32)
    for head in range(2):
        part = rotated(acc[:, head * DH:(head + 1) * DH], cosine[...], sine[...]).astype(BF)
        for block in range(2):
            out[block, head] = part[block * BLK:(block + 1) * BLK]


def whole(shape):
    return pl.BlockSpec(shape, lambda *_: (0,) * len(shape))


def project_kv(x0, x1, w, down, up, cosine, sine):
    width = x0.shape[1]
    rank = down.shape[1]
    return pl.pallas_call(
        kv_kernel,
        grid=(2,),
        in_specs=[
            whole((BLK, width)),
            whole((BLK, width)),
            pl.BlockSpec((width, 2 * DH), lambda j: (0, 4 + j)),
            whole((width, rank)),
            pl.BlockSpec((rank, 2 * DH), lambda j: (0, 4 + j)),
            whole((2 * BLK, DH)),
            whole((2 * BLK, DH)),
        ],
        out_specs=[
            pl.BlockSpec((2, 2, 1, BLK, DH), lambda j: (0, 0, j, 0, 0)),
            whole((2 * BLK, rank)),
        ],
        out_shape=[
            jax.ShapeDtypeStruct((2, 2, 2, BLK, DH), BF),
            jax.ShapeDtypeStruct((2 * BLK, rank), BF),
        ],
        scratch_shapes=[pltpu.VMEM((2 * BLK, width), BF), pltpu.VMEM((2 * BLK, rank), BF)],
        compiler_params=pltpu.CompilerParams(vmem_limit_bytes=40 * 2**20),
        cost_estimate=pl.CostEstimate(
            flops=2 * 2 * BLK * width * 4 * DH, bytes_accessed=width * 4 * DH * 2, transcendentals=0
        ),
        name="project_kv",
    )(x0, x1, w, down, up, cosine, sine)


def project_q(x0, x1, mid, w, up, cosine, sine):
    width = x0.shape[1]
    rank = mid.shape[1]
    return pl.pallas_call(
        q_kernel,
        grid=(4,),
        in_specs=[
            whole((BLK, width)),
            whole((BLK, width)),
            whole((2 * BLK, rank)),
            pl.BlockSpec((width, 2 * DH), lambda j: (0, j)),
            pl.BlockSpec((rank, 2 * DH), lambda j: (0, j)),
            whole((2 * BLK, DH)),
            whole((2 * BLK, DH)),
        ],
        out_specs=pl.BlockSpec((2, 2, BLK, DH), lambda j: (0, j, 0, 0)),
        out_shape=jax.ShapeDtypeStruct((2, 8, BLK, DH), BF),
        scratch_shapes=[pltpu.VMEM((2 * BLK, width), BF)],
        compiler_params=pltpu.CompilerParams(vmem_limit_bytes=40 * 2**20),
        cost_estimate=pl.CostEstimate(
            flops=2 * 2 * BLK * width * 8 * DH, bytes_accessed=width * 8 * DH * 2, transcendentals=0
        ),
        name="project_q",
    )(x0, x1, mid, w, up, cosine, sine)


def sort_kernel(source, a, b, c, d, out):
    for slot in range(H):
        pick = source[slot]
        which = pick // 8
        inner = pick % 8
        for k, ref in enumerate((a, b, c, d)):

            @pl.when(which == k)
            def _(ref=ref):
                out[slot // 4, slot % 4] = ref[inner]


def sort_heads(source, parts):
    return pl.pallas_call(
        sort_kernel,
        in_specs=[pl.BlockSpec(memory_space=pltpu.SMEM)] + [pl.BlockSpec(memory_space=pltpu.VMEM)] * 4,
        out_specs=pl.BlockSpec(memory_space=pltpu.VMEM),
        out_shape=jax.ShapeDtypeStruct((KV, 4, BLK, DH), BF),
        compiler_params=pltpu.CompilerParams(vmem_limit_bytes=16 * 2**20),
        cost_estimate=pl.CostEstimate(flops=0, bytes_accessed=2 * H * BLK * DH * 2, transcendentals=0),
        name="sort_heads",
    )(source, *parts)


def unsort_kernel(slots, a, out):
    for head in range(H):
        slot = slots[head]
        out[:, head * DH:(head + 1) * DH] = a[slot // 4, slot % 4]


def unsort_heads(slots, a):
    return pl.pallas_call(
        unsort_kernel,
        in_specs=[pl.BlockSpec(memory_space=pltpu.SMEM), pl.BlockSpec(memory_space=pltpu.VMEM)],
        out_specs=pl.BlockSpec(memory_space=pltpu.VMEM),
        out_shape=jax.ShapeDtypeStruct((BLK, H * DH), BF),
        compiler_params=pltpu.CompilerParams(vmem_limit_bytes=16 * 2**20),
        cost_estimate=pl.CostEstimate(flops=0, bytes_accessed=2 * H * BLK * DH * 2, transcendentals=0),
        name="unsort_heads",
    )(slots, a)


def attend_kernel(blocks, starts, own_half, q_ref, kv0, kv1, out, keys, values, sems, top, total, acc):
    tile = pl.program_id(0)
    yh = own_half[0]

    @pl.when(tile == 0)
    def _():
        copies = []
        for z in range(NZ):
            for yl in range(NYL):
                for kind, dst in enumerate((keys, values)):
                    for stage, src in enumerate((kv0, kv1)):
                        at_half = yh if stage == 0 else 1 - yh
                        at_low = yl if stage == 0 else 1 - yl
                        copies.append(
                            pltpu.make_async_copy(
                                src.at[:, yl, :, z, kind],
                                dst.at[pl.ds((z * NYL + at_low) * NX, NX), at_half],
                                sems.at[len(copies)],
                            )
                        )
        for copy in copies:
            copy.start()
        for copy in copies:
            copy.wait()

    rows = 4 * BLK
    block = blocks[tile]
    first = block * BLK
    last = first + BLK - 1

    def start_of(place):
        found = jnp.int32(0)
        for d in range(1, DOCS):
            found = jnp.maximum(found, jnp.where(starts[d] <= place, starts[d], 0))
        return found

    low = start_of(first) // KEYS
    high_start = start_of(last)
    diagonal = first // KEYS
    factor = (DH ** -0.5) * 1.4426950408889634

    top[...] = jnp.full(top.shape, NEG_BIG, F32)
    total[...] = jnp.zeros(total.shape, F32)
    acc[...] = jnp.zeros(acc.shape, F32)
    q = q_ref[0].reshape(rows, DH)

    def step(index, masked):
        k_tile = keys[index].reshape(KEYS, DH)
        v_tile = values[index].reshape(KEYS, DH)
        scores = lax.dot_general(q, k_tile, (((1,), (1,)), ((), ())), preferred_element_type=F32) * factor
        if masked:
            place = first + lax.broadcasted_iota(jnp.int32, (rows, 1), 0) % BLK
            begin = jnp.zeros((rows, 1), jnp.int32)
            for d in range(1, DOCS):
                begin = jnp.maximum(begin, jnp.where(place >= starts[d], starts[d], 0))
            at = index * KEYS + lax.broadcasted_iota(jnp.int32, (rows, KEYS), 1)
            scores = jnp.where((at <= place) & (at >= begin), scores, -jnp.inf)
        old = top[...]
        new = jnp.maximum(old, jnp.max(scores, axis=1, keepdims=True))
        shrink = jnp.exp2(old - new)
        powers = jnp.exp2(scores - new[:, :1])
        top[...] = new
        total[...] = total[...] * shrink + jnp.sum(powers, axis=1, keepdims=True)
        acc[...] = acc[...] * shrink + jnp.dot(powers.astype(BF), v_tile, preferred_element_type=F32)

    def body(index, carry):
        masked = (index == diagonal) | (index * KEYS < high_start)

        @pl.when(masked)
        def _():
            step(index, True)

        @pl.when(jnp.logical_not(masked))
        def _():
            step(index, False)

        return carry

    lax.fori_loop(low, diagonal + 1, body, 0)
    out[0] = (acc[...] / total[...]).astype(BF).reshape(4, BLK, DH)


def attend(blocks, starts, own_half, q, kv0, kv1):
    rows = 4 * BLK
    shape = (NX, NYL, NC, NZ, 2, BLK, DH)
    n_blocks = NZ * NYL * NX
    return pl.pallas_call(
        attend_kernel,
        grid=(8,),
        in_specs=[pl.BlockSpec(memory_space=pltpu.SMEM)] * 3
        + [
            pl.BlockSpec((1, 4, BLK, DH), lambda i: (i, 0, 0, 0)),
            pl.BlockSpec(memory_space=pl.ANY),
            pl.BlockSpec(memory_space=pl.ANY),
        ],
        out_specs=pl.BlockSpec((1, 4, BLK, DH), lambda i: (i, 0, 0, 0)),
        out_shape=jax.ShapeDtypeStruct((8, 4, BLK, DH), BF),
        scratch_shapes=[
            pltpu.VMEM((n_blocks, NYH, NC, BLK, DH), BF),
            pltpu.VMEM((n_blocks, NYH, NC, BLK, DH), BF),
            pltpu.SemaphoreType.DMA((32,)),
            pltpu.VMEM((rows, DH), F32),
            pltpu.VMEM((rows, DH), F32),
            pltpu.VMEM((rows, DH), F32),
        ],
        compiler_params=pltpu.CompilerParams(vmem_limit_bytes=40 * 2**20),
        cost_estimate=pl.CostEstimate(flops=10**10, bytes_accessed=10 * 2**20, transcendentals=10**7),
        name="attend",
    )(blocks, starts, own_half, q, kv0.reshape(shape), kv1.reshape(shape))


def per_device(tokens, w, down, up, document_index, query_to_key_head):
    z, yl, x, yh, c = (lax.axis_index(a) for a in ALL)
    block = flat(z, yl, x, yh, c)
    far_block = flat(z, 1 - yl, x, 1 - yh, c)
    other = 1 - 2 * c

    far = lax.ppermute(tokens, ALL, CROSS)
    near_pair = lax.ppermute(tokens, "c", SWAP)

    near_cos, near_sin = rope_tables(jnp.stack([block, block + other]))
    far_cos, far_sin = rope_tables(jnp.stack([far_block, far_block + other]))

    def spread_kv(kv):
        mine, theirs = kv[0], lax.ppermute(kv[1], "c", SWAP)
        heads = jnp.where(c == 0, jnp.concatenate([mine, theirs], 0), jnp.concatenate([theirs, mine], 0))
        heads = lax.all_to_all(heads, "z", split_axis=0, concat_axis=0, tiled=True)
        return lax.all_gather(heads[None], ("x", "yl", "c"), axis=0, tiled=True)

    kv_near, mid_near = project_kv(tokens, near_pair, w, down, up, near_cos, near_sin)
    kv0 = spread_kv(kv_near)
    q_near = project_q(tokens, near_pair, mid_near, w, up, near_cos, near_sin)

    far_pair = lax.ppermute(far, "c", SWAP)
    kv_far, mid_far = project_kv(far, far_pair, w, down, up, far_cos, far_sin)
    kv1 = spread_kv(kv_far)
    q_far = project_q(far, far_pair, mid_far, w, up, far_cos, far_sin)

    parts = (
        q_near[0],
        lax.ppermute(q_near[1], "c", SWAP),
        lax.ppermute(q_far[0], ALL, CROSS),
        lax.ppermute(q_far[1], ALL, CROSS_OTHER),
    )
    member = (query_to_key_head % 4) * 2 + query_to_key_head // 4
    heads = jnp.arange(H, dtype=jnp.int32)
    same = (member[None, :] == member[:, None]) & (heads[None, :] < heads[:, None])
    slots = member * 4 + jnp.sum(same.astype(jnp.int32), axis=1)
    source_of_head = ((heads // 8) ^ (yh * 2 + c)) * 8 + heads % 8
    source = jnp.sum(jnp.where(slots[None, :] == heads[:, None], source_of_head[None, :], 0), axis=1)
    sorted_q = sort_heads(source, parts)
    q = lax.all_to_all(sorted_q, ALL, split_axis=0, concat_axis=0, tiled=True, axis_index_groups=GROUPS)

    member_z = jnp.arange(8, dtype=jnp.int32) // 2
    member_yh = jnp.arange(8, dtype=jnp.int32) % 2
    blocks = flat(member_z, (yl ^ yh) ^ member_yh, (x - z + member_z) % NX, member_yh, c).astype(jnp.int32)
    starts = jnp.sum(
        (document_index[None, :] < jnp.arange(DOCS, dtype=jnp.int32)[:, None]).astype(jnp.int32), axis=1
    )
    context = attend(blocks, starts, yh[None].astype(jnp.int32), q, kv0, kv1)
    home = lax.all_to_all(context, ALL, split_axis=0, concat_axis=0, tiled=True, axis_index_groups=GROUPS)
    return unsort_heads(slots, home)


def solution(mesh):
    fine = Mesh(mesh.devices.reshape(NZ, NYL, NX, NYH, NC), ALL)
    return jax.shard_map(
        per_device,
        mesh=fine,
        in_specs=(P(ALL, None), P(None, ("yh", "c")), P(), P(None, ("yh", "c")), P(), P()),
        out_specs=P(ALL, None),
        check_vma=False,
    )
```

time: 429 us -> 222 us (0.52); the launches traced: 426 us -> 225 us
  matrix products: 141 us -> 0 us
  Pallas kernels: 0 us -> 77.9 us
  waiting for transfers between devices: 105 us -> 58.1 us
  local copies, waits for them, and re-layouts: 54.2 us -> 10.4 us
  other arithmetic: 33 us -> 5.39 us
  starting transfers between devices: 22.1 us -> 14 us
  loops' own time: 6.81 us -> 0 us
  blocking collectives: 50.2 us -> 45.3 us
    dot_general x45 -> x0, matrix products: 141 us -> none  [the longest x20 73.8 us: key_step(): jnp.einsum('qhd,khd->qhk', query_tile, key_tile, preferred_element_type=j...]
    pallas_call x0 -> x7, Pallas kernels: none -> 77.9 us  [the longest x1 52.6 us: attend(): pl.pallas_call(attend_kernel, grid=(8,), in_specs=[pl.BlockSpec(memory_sp...]
    all_gather x2, waiting for transfers between devices: 50.3 us -> 0.01 us  [spread_kv(): return lax.all_gather(heads[None], ('x', 'yl', 'c'), axis=0, tiled=True)]
    ppermute x0 -> x8, waiting for transfers between devices: none -> 37.9 us  [the longest x1 22.6 us: per_device(): far = lax.ppermute(tokens, ALL, CROSS)]
    all_to_all x5 -> x1, waiting for transfers between devices: 53.6 us -> 20.2 us  [per_device(): lax.all_to_all(sorted_q, ALL, split_axis=0, concat_axis=0, tiled=True, ax...]
    gather x1 -> x0, local copies, waits for them, and re-layouts: 23 us -> none  [per_device(): query_segments = jnp.take(document_index, query_places)]
    reduce_sum x20 -> x3, other arithmetic: 23.4 us -> 0.54 us  [the longest x1 0.25 us: per_device(): jnp.sum((document_index[None, :] < jnp.arange(DOCS, dtype=jnp.int32)[:, N...]
    all_to_all x5 -> x1, starting transfers between devices: 22.1 us -> 6.87 us  [per_device(): lax.all_to_all(sorted_q, ALL, split_axis=0, concat_axis=0, tiled=True, ax...]
  transfers between devices with their start and end apart: 7 -> 11, of which waited for: 6 -> 7; matrix products, arithmetic and copies ran while one was open for 11% -> 3% of each run, Pallas kernels for 0% -> 9%
where the time goes in v1:
time: 222 us; the launch traced here: 225 us
  Pallas kernels  77.9 us (35%)
  waiting for transfers between devices  58.1 us (26%)
  blocking collectives  45.3 us (20%)
  starting transfers between devices  14 us (6%)
  between operations  13.7 us (6%)
  local copies, waits for them, and re-layouts  10.4 us (5%)
  other arithmetic  5.39 us (2%)
    pallas_call x1, Pallas kernels, attend(): pl.pallas_call(attend_kernel, grid=(8,), in_specs=[pl.BlockSpec(memory_sp...  52.6 us
    all_to_all x2, blocking collectives, spread_kv(): heads = lax.all_to_all(heads, 'z', split_axis=0, concat_axis=0, tiled=True)  22.8 us
    ppermute x1, waiting for transfers between devices, per_device(): far = lax.ppermute(tokens, ALL, CROSS)  22.6 us
    all_to_all x1, blocking collectives, per_device(): lax.all_to_all(context, ALL, split_axis=0, concat_axis=0, tiled=True, axi...  22.5 us
    all_to_all x1, waiting for transfers between devices, per_device(): lax.all_to_all(sorted_q, ALL, split_axis=0, concat_axis=0, tiled=True, ax...  20.2 us
    pallas_call x2, Pallas kernels, project_q(): pl.pallas_call(q_kernel, grid=(4,), in_specs=[whole((BLK, width)), whole(...  12.3 us
    unnamed x41, local copies, waits for them, and re-layouts  9.64 us
    pallas_call x2, Pallas kernels, project_kv(): pl.pallas_call(kv_kernel, grid=(2,), in_specs=[whole((BLK, width)), whole...  8.55 us
  transfers between devices with their start and end apart: 11, of which 7 were waited for; matrix products, arithmetic and copies ran while one was open for 3% of the time, Pallas kernels for 9%

profile of v1, /device:TPU:0, one launch (start us, length us, event | category | flops | bytes accessed | tf_op | source)
XLA Modules:
  0.0 224.9 jit_solution(16370134894157184142)
XLA Ops:
  6.6 1.5 copy.11.down
  8.4 1.6 fusion.1
  10.2 1.3 copy-done
  12.3 4.1 %project_kv.2 = (bf16[2,2,2,128,128]{4,3,2,1,0:T(8,128)(2,1)S(1)}, bf16[256,64]{1,0:T(8,128)(2,1)S(1)}) custom-call(bf16[128,4096]{1,0:T(8,128)(2,1)S(1)} %copy-done, bf16[128,4096]{1,0:T(8,128)(2,1)S(1)} %collective-permute-done.x1, bf16[4096,1536]{1,0:T(8,128)(2,1)} %w.7, bf16[4096,64]{1,0:T(8,128)(2,1)S(1)} %copy.11.down, bf16[64,1536]{1,0:T(8,128)(2,1)S(1)} %copy-done.6, ...), custom_call_target="tpu_custom_call" | custom-call | flops 1073741824 | bytes 4194304 | tf_op jit(solution)/shard_map/project_kv/pallas_call | solution.py:115
  17.7 1.3 collective-permute-done.6
  20.1 12.5 %all_to_all.20 = bf16[4,2,128,128]{3,2,1,0:T(8,128)(2,1)} all-to-all(bf16[4,2,128,128]{3,2,1,0:T(8,128)(2,1)S(1)} %maximum_select_fusion), channel_id=1, replica_groups=mesh['z'=4,'yl'=2,'x'=4,'yh'=2,'c'=2] {'z'}, dimensions={0} | all-to-all | bytes 524288 | tf_op jit(solution)/shard_map/all_to_all | solution.py:338
  32.7 3.1 %collective-permute-start.2 = (bf16[128,4096]{1,0:T(8,128)(2,1)S(1)}, bf16[128,4096]{1,0:T(8,128)(2,1)S(1)}, u32[]{:S(2)}, u32[]{:S(2)}) collective-permute-start(bf16[128,4096]{1,0:T(8,128)(2,1)S(1)} %copy-done.1), channel_id=1, source_target_pairs={{0,18},{1,19},{2,16},{3,17},{4,22},{5,23},{6,20},{7,21},{8,26},{9,... | collective-permute-start | bytes 3145736 | tf_op jit(solution)/shard_map/ppermute | solution.py:329
  35.8 22.6 %collective-permute-done.2.x0 = bf16[128,4096]{1,0:T(8,128)(2,1)S(1)} collective-permute-done((bf16[128,4096]{1,0:T(8,128)(2,1)S(1)}, bf16[128,4096]{1,0:T(8,128)(2,1)S(1)}, u32[]{:S(2)}, u32[]{:S(2)}) %collective-permute-start.2) | collective-permute-done | bytes 1048608 | tf_op jit(solution)/shard_map/ppermute | solution.py:329
  58.4 1.6 pad_maximum_fusion.2
  61.0 4.4 %project_kv.3 = (bf16[2,2,2,128,128]{4,3,2,1,0:T(8,128)(2,1)S(1)}, bf16[256,64]{1,0:T(8,128)(2,1)S(1)}) custom-call(bf16[128,4096]{1,0:T(8,128)(2,1)S(1)} %collective-permute-done.2.x0, bf16[128,4096]{1,0:T(8,128)(2,1)S(1)} %collective-permute-done.3.x1, bf16[4096,1536]{1,0:T(8,128)(2,1)} %w.7, bf16[4096,64]{1,0:T(8,128)(2,1)S(1)} %copy.11.down, ...), custom_call_target="tpu_custom_call" | custom-call | flops 1073741824 | bytes 4194304 | tf_op jit(solution)/shard_map/project_kv/pallas_call | solution.py:115
  67.5 10.3 %all_to_all.21 = bf16[4,2,128,128]{3,2,1,0:T(8,128)(2,1)} all-to-all(bf16[4,2,128,128]{3,2,1,0:T(8,128)(2,1)S(1)} %maximum_select_fusion.1), channel_id=1, replica_groups=mesh['z'=4,'yl'=2,'x'=4,'yh'=2,'c'=2] {'z'}, dimensions={0} | all-to-all | bytes 524288 | tf_op jit(solution)/shard_map/all_to_all | solution.py:338
  79.0 6.2 %project_q.2 = bf16[2,8,128,128]{3,2,1,0:T(8,128)(2,1)S(1)} custom-call(bf16[128,4096]{1,0:T(8,128)(2,1)S(1)} %copy-done.1, bf16[128,4096]{1,0:T(8,128)(2,1)S(1)} %collective-permute-done.x1, bf16[256,64]{1,0:T(8,128)(2,1)S(1)} %get-tuple-element.9.mid, bf16[4096,1536]{1,0:T(8,128)(2,1)} %w.7, bf16[64,1536]{1,0:T(8,128)(2,1)S(1)} %copy-done.7, ...), custom_call_target="tpu_custom_call" | custom-call | flops 2147483648 | bytes 8388608 | tf_op jit(solution)/shard_map/project_q/pallas_call | solution.py:147
  85.4 6.2 %project_q.3 = bf16[2,8,128,128]{3,2,1,0:T(8,128)(2,1)S(1)} custom-call(bf16[128,4096]{1,0:T(8,128)(2,1)S(1)} %copy-done.3, bf16[128,4096]{1,0:T(8,128)(2,1)S(1)} %copy-done.5, bf16[256,64]{1,0:T(8,128)(2,1)S(1)} %copy-done.15, bf16[4096,1536]{1,0:T(8,128)(2,1)} %w.7, bf16[64,1536]{1,0:T(8,128)(2,1)S(1)} %copy-done.7, f32[256,128]{1,0:T(8,128)S(1)} %copy-done.11, ...), custom_call_target="tpu_custom_call" | custom-call | flops 2147483648 | bytes 8388608 | tf_op jit(solution)/shard_map/project_q/pallas_call | solution.py:147
  91.6 3.1 %collective-permute-start.4 = (bf16[8,128,128]{2,1,0:T(8,128)(2,1)S(1)}, bf16[8,128,128]{2,1,0:T(8,128)(2,1)S(1)}, u32[]{:S(2)}, u32[]{:S(2)}) collective-permute-start(bf16[8,128,128]{2,1,0:T(8,128)(2,1)S(1)} %get-tuple-element.14), channel_id=1, source_target_pairs={{0,18},{1,19},{2,16},{3,17},{4,22},{5,23},{6,20},{7,21},{8,26},{9,... | collective-permute-start | bytes 786440 | tf_op jit(solution)/shard_map/ppermute | solution.py:353
  95.0 7.0 %collective-permute-done.4.c = bf16[8,128,128]{2,1,0:T(8,128)(2,1)S(1)} collective-permute-done((bf16[8,128,128]{2,1,0:T(8,128)(2,1)S(1)}, bf16[8,128,128]{2,1,0:T(8,128)(2,1)S(1)}, u32[]{:S(2)}, u32[]{:S(2)}) %collective-permute-start.4) | collective-permute-done | bytes 262176 | tf_op jit(solution)/shard_map/ppermute | solution.py:353
  102.0 4.8 %collective-permute-done.5.d = bf16[8,128,128]{2,1,0:T(8,128)(2,1)S(1)} collective-permute-done((bf16[8,128,128]{2,1,0:T(8,128)(2,1)S(1)}, bf16[8,128,128]{2,1,0:T(8,128)(2,1)S(1)}, u32[]{:S(2)}, u32[]{:S(2)}) %collective-permute-start.5) | collective-permute-done | bytes 262176 | tf_op jit(solution)/shard_map/ppermute | solution.py:354
  106.8 2.5 %sort_heads.1 = bf16[8,4,128,128]{3,2,1,0:T(8,128)(2,1)} custom-call(s32[32]{0:T(128)S(1)} %select_reduce_fusion.source, bf16[8,128,128]{2,1,0:T(8,128)(2,1)S(1)} %get-tuple-element.16.a, bf16[8,128,128]{2,1,0:T(8,128)(2,1)S(1)} %collective-permute-done.1.b, bf16[8,128,128]{2,1,0:T(8,128)(2,1)S(1)} %collective-permute-done.4.c, ...), custom_call_target="tpu_custom_call" | custom-call | bytes 2097152 | tf_op jit(solution)/shard_map/sort_heads/pallas_call | solution.py:183
  109.3 6.9 %all-to-all-start = ((bf16[8,4,128,128]{3,2,1,0:T(8,128)(2,1)}), bf16[8,4,128,128]{3,2,1,0:T(8,128)(2,1)S(1)}, u32[]{:S(2)}, u32[]{:S(2)}) async-start(bf16[8,4,128,128]{3,2,1,0:T(8,128)(2,1)} %sort_heads.1), calls=%async_computation | async-start | bytes 2097152 | tf_op jit(solution)/shard_map/all_to_all | solution.py:363
  116.5 20.2 %all-to-all-done.q_ref = bf16[8,4,128,128]{3,2,1,0:T(8,128)(2,1)S(1)} async-done(((bf16[8,4,128,128]{3,2,1,0:T(8,128)(2,1)}), bf16[8,4,128,128]{3,2,1,0:T(8,128)(2,1)S(1)}, u32[]{:S(2)}, u32[]{:S(2)}) %all-to-all-start) | async-done | bytes 1048608 | tf_op jit(solution)/shard_map/all_to_all | solution.py:363
  136.6 2.2 copy-done.16
  138.8 2.2 copy-done.17
  141.0 52.6 %attend.1 = bf16[8,4,128,128]{3,2,1,0:T(8,128)(2,1)S(1)} custom-call(s32[8]{0:T(128)S(1)} %multiply_add_fusion.blocks, s32[4]{0:T(128)S(1)} %convert_reduce_fusion.starts, s32[1]{0:T(128)} %bitcast.own_half, bf16[8,4,128,128]{3,2,1,0:T(8,128)(2,1)S(1)} %all-to-all-done.q_ref, bf16[4,2,2,4,2,128,128]{6,5,4,3,2,1,0:T(8,128)(2,1)S(1)} %bitcast.27, ...), custom_call_target="tpu_custom_call" | custom-call | flops 10000000000 | bytes 10485760 | tf_op jit(solution)/shard_map/attend/pallas_call | solution.py:298
  193.7 22.5 %all_to_all.22.a = bf16[8,4,128,128]{3,2,1,0:T(8,128)(2,1)S(1)} all-to-all(bf16[8,4,128,128]{3,2,1,0:T(8,128)(2,1)S(1)} %attend.1), channel_id=1, replica_groups={{0,18,36,54,72,90,108,126},{1,19,37,55,73,91,109,127},{16,2,52,38,88,74..., dimensions={0} | all-to-all | bytes 2097152 | tf_op jit(solution)/shard_map/all_to_all | solution.py:372
  216.2 1.9 unsort_heads.1
  (72 shorter events, 8.7 us)
Async XLA Ops:
  6.5 130.1 %all-gather.5.cloned.1.call-start = ((), (), s32[]{:S(2)}) async-start(), calls=%async_computation.4 | async-start | bytes 4456448 | tf_op jit(solution)/shard_map/all_gather | solution.py:339
  6.5 3.6 %collective-permute-start = (bf16[128,4096]{1,0:T(8,128)(2,1)}, bf16[128,4096]{1,0:T(8,128)(2,1)S(1)}, u32[]{:S(2)}, u32[]{:S(2)}) collective-permute-start(bf16[128,4096]{1,0:T(8,128)(2,1)} %x0.3), channel_id=1, source_target_pairs={{0,1},{1,0},{2,3},{3,2},{4,5},{5,4},{6,7},{7,6},{8,9},{9,8},{10,11... | collective-permute-start | bytes 3145736 | tf_op jit(solution)/shard_map/ppermute | solution.py:330
  10.1 6.3 %copy-start.8 = (f32[256,128]{1,0:T(8,128)}, f32[256,128]{1,0:T(8,128)S(1)}, u32[]{:S(2)}) copy-start(f32[256,128]{1,0:T(8,128)S(1)} %get-tuple-element.31.sine) | copy-start | bytes 393220
  12.3 20.4 %copy-start.1 = (bf16[128,4096]{1,0:T(8,128)(2,1)S(1)}, bf16[128,4096]{1,0:T(8,128)(2,1)}, u32[]{:S(2)}) copy-start(bf16[128,4096]{1,0:T(8,128)(2,1)} %x0.3) | copy-start | bytes 3145732
  12.3 48.7 %copy-start.7 = (bf16[64,1536]{1,0:T(8,128)(2,1)S(1)}, bf16[64,1536]{1,0:T(8,128)(2,1)}, u32[]{:S(2)}) copy-start(bf16[64,1536]{1,0:T(8,128)(2,1)} %up.7) | copy-start | bytes 589828
  17.2 1.8 collective-permute-start.6
  32.7 104.0 %all-gather.7.cloned.1.call-start = ((), (), s32[]{:S(2)}) async-start(), calls=%async_computation.5 | async-start | bytes 4456448 | tf_op jit(solution)/shard_map/all_gather | solution.py:339
  32.7 25.6 %collective-permute-start.2 = (bf16[128,4096]{1,0:T(8,128)(2,1)S(1)}, bf16[128,4096]{1,0:T(8,128)(2,1)S(1)}, u32[]{:S(2)}, u32[]{:S(2)}) collective-permute-start(bf16[128,4096]{1,0:T(8,128)(2,1)S(1)} %copy-done.1), channel_id=1, source_target_pairs={{0,18},{1,19},{2,16},{3,17},{4,22},{5,23},{6,20},{7,21},{8,26},{9,... | collective-permute-start | bytes 3145736 | tf_op jit(solution)/shard_map/ppermute | solution.py:329
  58.4 7.1 %copy-start.2 = (bf16[128,4096]{1,0:T(8,128)(2,1)}, bf16[128,4096]{1,0:T(8,128)(2,1)S(1)}, u32[]{:S(2)}) copy-start(bf16[128,4096]{1,0:T(8,128)(2,1)S(1)} %collective-permute-done.2.x0) | copy-start | bytes 3145732
  58.4 2.7 %collective-permute-start.3 = (bf16[128,4096]{1,0:T(8,128)(2,1)S(1)}, bf16[128,4096]{1,0:T(8,128)(2,1)S(1)}, u32[]{:S(2)}, u32[]{:S(2)}) collective-permute-start(bf16[128,4096]{1,0:T(8,128)(2,1)S(1)} %collective-permute-done.2.x0), channel_id=1, source_target_pairs={{0,1},{1,0},{2,3},{3,2},{4,5},{5,4},{6,7},{7,6},{8,9},{9,8},{10,11... | collective-permute-start | bytes 3145736 | tf_op jit(solution)/shard_map/ppermute | solution.py:345
  60.0 5.5 %copy-start.10 = (f32[256,128]{1,0:T(8,128)}, f32[256,128]{1,0:T(8,128)S(1)}, u32[]{:S(2)}) copy-start(f32[256,128]{1,0:T(8,128)S(1)} %get-tuple-element.32.cosine) | copy-start | bytes 393220
  60.0 5.5 %copy-start.12 = (f32[256,128]{1,0:T(8,128)}, f32[256,128]{1,0:T(8,128)S(1)}, u32[]{:S(2)}) copy-start(f32[256,128]{1,0:T(8,128)S(1)} %get-tuple-element.33.sine) | copy-start | bytes 393220
  61.0 16.9 %copy-start.19 = (s32[32]{0:T(128)S(1)}, s32[32]{0:T(128)}, u32[]{:S(2)}) copy-start(s32[32]{0:T(128)} %param.11) | copy-start | bytes 388
  66.1 1.3 collective-permute-start.7
  79.0 6.3 %copy-start.3 = (bf16[128,4096]{1,0:T(8,128)(2,1)S(1)}, bf16[128,4096]{1,0:T(8,128)(2,1)}, u32[]{:S(2)}) copy-start(bf16[128,4096]{1,0:T(8,128)(2,1)} %copy-done.2) | copy-start | bytes 3145732
  79.0 6.3 %copy-start.5 = (bf16[128,4096]{1,0:T(8,128)(2,1)S(1)}, bf16[128,4096]{1,0:T(8,128)(2,1)}, u32[]{:S(2)}) copy-start(bf16[128,4096]{1,0:T(8,128)(2,1)} %copy-done.4) | copy-start | bytes 3145732
  79.0 6.3 %copy-start.11 = (f32[256,128]{1,0:T(8,128)S(1)}, f32[256,128]{1,0:T(8,128)}, u32[]{:S(2)}) copy-start(f32[256,128]{1,0:T(8,128)} %copy-done.10) | copy-start | bytes 393220
  79.0 6.3 %copy-start.13 = (f32[256,128]{1,0:T(8,128)S(1)}, f32[256,128]{1,0:T(8,128)}, u32[]{:S(2)}) copy-start(f32[256,128]{1,0:T(8,128)} %copy-done.12) | copy-start | bytes 393220
  79.0 6.3 %copy-start.15 = (bf16[256,64]{1,0:T(8,128)(2,1)S(1)}, bf16[256,64]{1,0:T(8,128)(2,1)}, u32[]{:S(2)}) copy-start(bf16[256,64]{1,0:T(8,128)(2,1)} %copy-done.14) | copy-start | bytes 98308
  85.2 9.8 %collective-permute-start.1 = (bf16[8,128,128]{2,1,0:T(8,128)(2,1)S(1)}, bf16[8,128,128]{2,1,0:T(8,128)(2,1)S(1)}, u32[]{:S(2)}, u32[]{:S(2)}) collective-permute-start(bf16[8,128,128]{2,1,0:T(8,128)(2,1)S(1)} %get-tuple-element.15), channel_id=1, source_target_pairs={{0,1},{1,0},{2,3},{3,2},{4,5},{5,4},{6,7},{7,6},{8,9},{9,8},{10,11... | collective-permute-start | bytes 786440 | tf_op jit(solution)/shard_map/ppermute | solution.py:352
  91.6 24.7 %copy-start.18 = (s32[16384]{0:T(1024)S(1)}, s32[16384]{0:T(1024)}, u32[]{:S(2)}) copy-start(s32[16384]{0:T(1024)} %param.10) | copy-start | bytes 196612
  91.6 10.4 %collective-permute-start.4 = (bf16[8,128,128]{2,1,0:T(8,128)(2,1)S(1)}, bf16[8,128,128]{2,1,0:T(8,128)(2,1)S(1)}, u32[]{:S(2)}, u32[]{:S(2)}) collective-permute-start(bf16[8,128,128]{2,1,0:T(8,128)(2,1)S(1)} %get-tuple-element.14), channel_id=1, source_target_pairs={{0,18},{1,19},{2,16},{3,17},{4,22},{5,23},{6,20},{7,21},{8,26},{9,... | collective-permute-start | bytes 786440 | tf_op jit(solution)/shard_map/ppermute | solution.py:353
  94.7 12.1 %collective-permute-start.5 = (bf16[8,128,128]{2,1,0:T(8,128)(2,1)S(1)}, bf16[8,128,128]{2,1,0:T(8,128)(2,1)S(1)}, u32[]{:S(2)}, u32[]{:S(2)}) collective-permute-start(bf16[8,128,128]{2,1,0:T(8,128)(2,1)S(1)} %get-tuple-element.13), channel_id=1, source_target_pairs={{0,19},{1,18},{2,17},{3,16},{4,23},{5,22},{6,21},{7,20},{8,27},{9,... | collective-permute-start | bytes 786440 | tf_op jit(solution)/shard_map/ppermute | solution.py:354
  109.3 27.3 %all-to-all-start = ((bf16[8,4,128,128]{3,2,1,0:T(8,128)(2,1)}), bf16[8,4,128,128]{3,2,1,0:T(8,128)(2,1)S(1)}, u32[]{:S(2)}, u32[]{:S(2)}) async-start(bf16[8,4,128,128]{3,2,1,0:T(8,128)(2,1)} %sort_heads.1), calls=%async_computation | async-start | bytes 2097152 | tf_op jit(solution)/shard_map/all_to_all | solution.py:363
  (7 other events, 12.6 us)
Sparse Core Ops, SparseCore 0:
  32.8 36.8 all-gather.4
  78.0 36.5 all-gather.6

commit v2 on v1

--- a/solution.py
+++ b/solution.py
@@ -21,7 +21,7 @@
 ALL = ("z", "yl", "x", "yh", "c")
 BF = jnp.bfloat16
 F32 = jnp.float32
-KEYS = 512
+WIDE = 8
 
 
 def flat(z, yl, x, yh, c):
@@ -209,115 +209,149 @@
     )(slots, a)
 
 
-def attend_kernel(blocks, starts, own_half, q_ref, kv0, kv1, out, keys, values, sems, top, total, acc):
-    tile = pl.program_id(0)
-    yh = own_half[0]
-
-    @pl.when(tile == 0)
-    def _():
-        copies = []
-        for z in range(NZ):
-            for yl in range(NYL):
-                for kind, dst in enumerate((keys, values)):
-                    for stage, src in enumerate((kv0, kv1)):
-                        at_half = yh if stage == 0 else 1 - yh
-                        at_low = yl if stage == 0 else 1 - yl
-                        copies.append(
-                            pltpu.make_async_copy(
-                                src.at[:, yl, :, z, kind],
-                                dst.at[pl.ds((z * NYL + at_low) * NX, NX), at_half],
-                                sems.at[len(copies)],
-                            )
-                        )
-        for copy in copies:
+def attend_kernel(blocks, starts, own, q_ref, kv0, kv1, out, pairs, sems, top, total, acc, floor):
+    yh = own[0]
+
+    def copies_of(z):
+        return [
+            pltpu.make_async_copy(src.at[:, pl.ds((own[1] - z + NZ) % NZ, 1)], pairs.at[stage, :, pl.ds(z, 1)], sems.at[2 * z + stage])
+            for stage, src in enumerate((kv0, kv1))
+        ]
+
+    for z in range(NZ):
+        for copy in copies_of(z):
             copy.start()
-        for copy in copies:
+
+    def gathered(begin_block, width, kind):
+        parts = []
+        for k in range(width):
+            key_block = jnp.maximum(begin_block + k, 0)
+            low = (key_block // (NC * NYH * NX)) % NYL
+            stage = ((key_block // NC) % NYH) ^ yh
+            source = (((key_block // (NC * NYH)) % NX) * NYL + (low ^ stage)) * NC + key_block % NC
+            parts.append(pairs[stage, source, key_block // (NC * NYH * NX * NYL), kind])
+        return jnp.concatenate(parts, axis=0)
+
+    def one_tile(tile):
+        rows = 4 * BLK
+        block = blocks[tile]
+        first = block * BLK
+
+        def start_of(place):
+            found = jnp.int32(0)
+            for d in range(1, DOCS):
+                found = jnp.maximum(found, jnp.where(starts[d] <= place, starts[d], 0))
+            return found
+
+        span = block + 1 - start_of(first) // BLK
+        latest_start = start_of(first + BLK - 1)
+        factor = (DH ** -0.5) * 1.4426950408889634
+
+        top[...] = jnp.full(top.shape, NEG_BIG, F32)
+        total[...] = jnp.zeros(total.shape, F32)
+        acc[...] = jnp.zeros(acc.shape, F32)
+        q = q_ref[tile].reshape(rows, DH)
+
+        place = first + lax.broadcasted_iota(jnp.int32, (rows, DH), 0) % BLK
+        begin = jnp.zeros((rows, DH), jnp.int32)
+        for d in range(1, DOCS):
+            begin = jnp.maximum(begin, jnp.where(place >= starts[d], starts[d], 0))
+        floor[...] = begin
+
+        def step(begin_block, width, at_end, at_start):
+            k_tile = gathered(begin_block, width, 0)
+            v_tile = gathered(begin_block, width, 1)
+            scores = lax.dot_general(q, k_tile, (((1,), (1,)), ((), ())), preferred_element_type=F32)
+            parts = [scores[:, j:j + DH] * factor for j in range(0, width * BLK, DH)]
+            lane = lax.broadcasted_iota(jnp.int32, (rows, DH), 1)
+            if at_start:
+                lowest = floor[...] - lane
+                parts = [jnp.where(lowest <= (begin_block + j) * BLK, part, -jnp.inf) for j, part in enumerate(parts)]
+            if at_end:
+                inside = lane <= lax.broadcasted_iota(jnp.int32, (rows, DH), 0) % BLK
+                parts[-1] = jnp.where(inside, parts[-1], -jnp.inf)
+            old = top[...]
+            peak = functools.reduce(jnp.maximum, parts)
+            new = jnp.maximum(old, jnp.max(peak, axis=1, keepdims=True))
+            shrink = jnp.exp2(old - new)
+            powers = [jnp.exp2(part - new) for part in parts]
+            top[...] = new
+            total[...] = total[...] * shrink + functools.reduce(jnp.add, powers)
+            weights = jnp.concatenate([p.astype(BF) for p in powers], axis=1)
+            acc[...] = acc[...] * shrink + jnp.dot(weights, v_tile, preferred_element_type=F32)
+
+        whole_steps = (span + WIDE // 2 - 1) // WIDE
+
+        def starting(begin_block):
+            return begin_block * BLK < latest_start
+
+        def either(begin_block, width, at_end):
+            early = starting(begin_block)
+
+            @pl.when(early)
+            def _():
+                step(begin_block, width, at_end, True)
+
+            @pl.when(jnp.logical_not(early))
+            def _():
+                step(begin_block, width, at_end, False)
+
+        @pl.when(whole_steps > 0)
+        def _():
+            either(block + 1 - WIDE, WIDE, True)
+
+        def body(index, carry):
+            either(block + 1 - WIDE * (index + 1), WIDE, False)
+            return carry
+
+        lax.fori_loop(1, whole_steps, body, 0)
+
+        left = span - WIDE * whole_steps
+
+        @pl.when((left > 0) & (whole_steps == 0))
+        def _():
+            step(block + 1 - WIDE // 2, WIDE // 2, True, True)
+
+        @pl.when((left > 0) & (whole_steps > 0))
+        def _():
+            step(block + 1 - WIDE * whole_steps - WIDE // 2, WIDE // 2, False, True)
+
+        out[tile] = (acc[...] / jnp.sum(total[...], axis=1, keepdims=True)).astype(BF).reshape(4, BLK, DH)
+
+    def pair(z, carry):
+        for copy in copies_of(z):
             copy.wait()
-
+        one_tile(2 * z)
+        one_tile(2 * z + 1)
+        return carry
+
+    lax.fori_loop(0, NZ, pair, 0)
+
+
+def attend(blocks, starts, own, q, kv0, kv1):
     rows = 4 * BLK
-    block = blocks[tile]
-    first = block * BLK
-    last = first + BLK - 1
-
-    def start_of(place):
-        found = jnp.int32(0)
-        for d in range(1, DOCS):
-            found = jnp.maximum(found, jnp.where(starts[d] <= place, starts[d], 0))
-        return found
-
-    low = start_of(first) // KEYS
-    high_start = start_of(last)
-    diagonal = first // KEYS
-    factor = (DH ** -0.5) * 1.4426950408889634
-
-    top[...] = jnp.full(top.shape, NEG_BIG, F32)
-    total[...] = jnp.zeros(total.shape, F32)
-    acc[...] = jnp.zeros(acc.shape, F32)
-    q = q_ref[0].reshape(rows, DH)
-
-    def step(index, masked):
-        k_tile = keys[index].reshape(KEYS, DH)
-        v_tile = values[index].reshape(KEYS, DH)
-        scores = lax.dot_general(q, k_tile, (((1,), (1,)), ((), ())), preferred_element_type=F32) * factor
-        if masked:
-            place = first + lax.broadcasted_iota(jnp.int32, (rows, 1), 0) % BLK
-            begin = jnp.zeros((rows, 1), jnp.int32)
-            for d in range(1, DOCS):
-                begin = jnp.maximum(begin, jnp.where(place >= starts[d], starts[d], 0))
-            at = index * KEYS + lax.broadcasted_iota(jnp.int32, (rows, KEYS), 1)
-            scores = jnp.where((at <= place) & (at >= begin), scores, -jnp.inf)
-        old = top[...]
-        new = jnp.maximum(old, jnp.max(scores, axis=1, keepdims=True))
-        shrink = jnp.exp2(old - new)
-        powers = jnp.exp2(scores - new[:, :1])
-        top[...] = new
-        total[...] = total[...] * shrink + jnp.sum(powers, axis=1, keepdims=True)
-        acc[...] = acc[...] * shrink + jnp.dot(powers.astype(BF), v_tile, preferred_element_type=F32)
-
-    def body(index, carry):
-        masked = (index == diagonal) | (index * KEYS < high_start)
-
-        @pl.when(masked)
-        def _():
-            step(index, True)
-
-        @pl.when(jnp.logical_not(masked))
-        def _():
-            step(index, False)
-
-        return carry
-
-    lax.fori_loop(low, diagonal + 1, body, 0)
-    out[0] = (acc[...] / total[...]).astype(BF).reshape(4, BLK, DH)
-
-
-def attend(blocks, starts, own_half, q, kv0, kv1):
-    rows = 4 * BLK
-    shape = (NX, NYL, NC, NZ, 2, BLK, DH)
-    n_blocks = NZ * NYL * NX
     return pl.pallas_call(
         attend_kernel,
-        grid=(8,),
         in_specs=[pl.BlockSpec(memory_space=pltpu.SMEM)] * 3
         + [
-            pl.BlockSpec((1, 4, BLK, DH), lambda i: (i, 0, 0, 0)),
+            pl.BlockSpec(memory_space=pltpu.VMEM),
             pl.BlockSpec(memory_space=pl.ANY),
             pl.BlockSpec(memory_space=pl.ANY),
         ],
-        out_specs=pl.BlockSpec((1, 4, BLK, DH), lambda i: (i, 0, 0, 0)),
+        out_specs=pl.BlockSpec(memory_space=pltpu.VMEM),
         out_shape=jax.ShapeDtypeStruct((8, 4, BLK, DH), BF),
         scratch_shapes=[
-            pltpu.VMEM((n_blocks, NYH, NC, BLK, DH), BF),
-            pltpu.VMEM((n_blocks, NYH, NC, BLK, DH), BF),
-            pltpu.SemaphoreType.DMA((32,)),
+            pltpu.VMEM((2, NX * NYL * NC, NZ, 2, BLK, DH), BF),
+            pltpu.SemaphoreType.DMA((2 * NZ,)),
             pltpu.VMEM((rows, DH), F32),
             pltpu.VMEM((rows, DH), F32),
             pltpu.VMEM((rows, DH), F32),
-        ],
-        compiler_params=pltpu.CompilerParams(vmem_limit_bytes=40 * 2**20),
+            pltpu.VMEM((rows, DH), jnp.int32),
+        ],
+        compiler_params=pltpu.CompilerParams(vmem_limit_bytes=60 * 2**20),
         cost_estimate=pl.CostEstimate(flops=10**10, bytes_accessed=10 * 2**20, transcendentals=10**7),
         name="attend",
-    )(blocks, starts, own_half, q, kv0.reshape(shape), kv1.reshape(shape))
+    )(blocks, starts, own, q, kv0, kv1)
 
 
 def per_device(tokens, w, down, up, document_index, query_to_key_head):
@@ -332,19 +366,27 @@
     near_cos, near_sin = rope_tables(jnp.stack([block, block + other]))
     far_cos, far_sin = rope_tables(jnp.stack([far_block, far_block + other]))
 
-    def spread_kv(kv):
+    def split_kv(kv):
         mine, theirs = kv[0], lax.ppermute(kv[1], "c", SWAP)
         heads = jnp.where(c == 0, jnp.concatenate([mine, theirs], 0), jnp.concatenate([theirs, mine], 0))
-        heads = lax.all_to_all(heads, "z", split_axis=0, concat_axis=0, tiled=True)
-        return lax.all_gather(heads[None], ("x", "yl", "c"), axis=0, tiled=True)
+        rows = []
+        for k in range(NZ):
+            head = lax.dynamic_index_in_dim(heads, (z + k) % NZ, 0, keepdims=False)
+            rows.append(lax.ppermute(head, "z", [(i, (i + k) % NZ) for i in range(NZ)]) if k else head)
+        return jnp.stack(rows)[None]
+
+    def spread_kv(rows):
+        return lax.all_gather(rows, ("x", "yl", "c"), axis=0, tiled=True)
 
     kv_near, mid_near = project_kv(tokens, near_pair, w, down, up, near_cos, near_sin)
-    kv0 = spread_kv(kv_near)
+    rows_near = split_kv(kv_near)
+    kv0 = spread_kv(rows_near)
     q_near = project_q(tokens, near_pair, mid_near, w, up, near_cos, near_sin)
 
+    far, q_near, rows_near = lax.optimization_barrier((far, q_near, rows_near))
     far_pair = lax.ppermute(far, "c", SWAP)
     kv_far, mid_far = project_kv(far, far_pair, w, down, up, far_cos, far_sin)
-    kv1 = spread_kv(kv_far)
+    kv1 = spread_kv(split_kv(kv_far))
     q_far = project_q(far, far_pair, mid_far, w, up, far_cos, far_sin)
 
     parts = (
@@ -368,7 +410,7 @@
     starts = jnp.sum(
         (document_index[None, :] < jnp.arange(DOCS, dtype=jnp.int32)[:, None]).astype(jnp.int32), axis=1
     )
-    context = attend(blocks, starts, yh[None].astype(jnp.int32), q, kv0, kv1)
+    context = attend(blocks, starts, jnp.stack([yh, z]).astype(jnp.int32), q, kv0, kv1)
     home = lax.all_to_all(context, ALL, split_axis=0, concat_axis=0, tiled=True, axis_index_groups=GROUPS)
     return unsort_heads(slots, home)
 

time: 222 us -> 195 us (0.88); the launches traced: 225 us -> 195 us
  Pallas kernels: 77.9 us -> 56.6 us
  blocking collectives: 45.3 us -> 24.6 us
  starting transfers between devices: 14 us -> 22.5 us
  waiting for transfers between devices: 58.1 us -> 61.6 us
    all_to_all x2 -> x0, blocking collectives: 22.8 us -> none  [spread_kv(): heads = lax.all_to_all(heads, 'z', split_axis=0, concat_axis=0, tiled=True)]
    pallas_call x1, Pallas kernels: 52.6 us -> 31.9 us  [attend(): pl.pallas_call(attend_kernel, in_specs=[pl.BlockSpec(memory_space=pltpu.S...]
    ppermute x2 -> x8, waiting for transfers between devices: 2.53 us -> 13.2 us  [the longest x6 10.6 us: split_kv(): lax.ppermute(head, 'z', [(i, (i + k) % NZ) for i in range(NZ)])]
    ppermute x2 -> x8, starting transfers between devices: 0.63 us -> 8.29 us  [the longest x6 7.56 us: split_kv(): lax.ppermute(head, 'z', [(i, (i + k) % NZ) for i in range(NZ)])]
    ppermute x1, waiting for transfers between devices: 22.6 us -> 16 us  [per_device(): far = lax.ppermute(tokens, ALL, CROSS)]
    unnamed x41 -> x31, local copies, waits for them, and re-layouts: 9.64 us -> 6.8 us
  transfers between devices with their start and end apart: 11 -> 17, of which waited for: 7 -> 13; matrix products, arithmetic and copies ran while one was open for 3% -> 4% of each run, Pallas kernels for 9% -> 10%
where the time goes in v2:
time: 195 us
  waiting for transfers between devices  61.6 us (32%)
  Pallas kernels  56.6 us (29%)
  blocking collectives  24.6 us (13%)
  starting transfers between devices  22.5 us (12%)
  between operations  13.7 us (7%)
  local copies, waits for them, and re-layouts  8.71 us (4%)
  other arithmetic  7.13 us (4%)
    pallas_call x1, Pallas kernels, attend(): pl.pallas_call(attend_kernel, in_specs=[pl.BlockSpec(memory_space=pltpu.S...  31.9 us
    all_to_all x1, blocking collectives, per_device(): lax.all_to_all(context, ALL, split_axis=0, concat_axis=0, tiled=True, axi...  24.6 us
    all_to_all x1, waiting for transfers between devices, per_device(): lax.all_to_all(sorted_q, ALL, split_axis=0, concat_axis=0, tiled=True, ax...  18 us
    ppermute x1, waiting for transfers between devices, per_device(): far = lax.ppermute(tokens, ALL, CROSS)  16 us
    pallas_call x2, Pallas kernels, project_q(): pl.pallas_call(q_kernel, grid=(4,), in_specs=[whole((BLK, width)), whole(...  12.1 us
    ppermute x6, waiting for transfers between devices, split_kv(): lax.ppermute(head, 'z', [(i, (i + k) % NZ) for i in range(NZ)])  10.6 us
    pallas_call x2, Pallas kernels, project_kv(): pl.pallas_call(kv_kernel, grid=(2,), in_specs=[whole((BLK, width)), whole...  8.15 us
    all_to_all x1, starting transfers between devices, per_device(): lax.all_to_all(sorted_q, ALL, split_axis=0, concat_axis=0, tiled=True, ax...  7.84 us
  transfers between devices with their start and end apart: 17, of which 13 were waited for; matrix products, arithmetic and copies ran while one was open for 4% of the time, Pallas kernels for 10%

profile of v2, /device:TPU:0, one launch (start us, length us, event | category | flops | bytes accessed | tf_op | source)
XLA Modules:
  0.0 194.8 jit_solution(2954522198194379709)
XLA Ops:
  6.6 1.5 copy.11.down
  8.3 1.6 fusion.1
  12.4 4.1 %project_kv.2 = (bf16[2,2,2,128,128]{4,3,2,1,0:T(8,128)(2,1)S(1)}, bf16[256,64]{1,0:T(8,128)(2,1)S(1)}) custom-call(bf16[128,4096]{1,0:T(8,128)(2,1)S(1)} %copy-done, bf16[128,4096]{1,0:T(8,128)(2,1)S(1)} %collective-permute-done.1.x1, bf16[4096,1536]{1,0:T(8,128)(2,1)} %w.7, bf16[4096,64]{1,0:T(8,128)(2,1)S(1)} %copy.11.down, ...), custom_call_target="tpu_custom_call" | custom-call | flops 1073741824 | bytes 4194304 | tf_op jit(solution)/shard_map/project_kv/pallas_call | solution.py:115
  17.7 1.3 collective-permute-done.2
  20.2 4.2 %collective-permute-start.5 = (bf16[2,128,128]{2,1,0:T(8,128)(2,1)S(1)}, bf16[2,128,128]{2,1,0:T(8,128)(2,1)S(1)}, u32[]{:S(2)}, u32[]{:S(2)}) collective-permute-start(bf16[2,128,128]{2,1,0:T(8,128)(2,1)S(1)} %get-tuple-element.28), channel_id=1, source_target_pairs={{0,96},{32,0},{64,32},{96,64},{1,97},{33,1},{65,33},{97,65},{2,98}... | collective-permute-start | bytes 196616 | tf_op jit(solution)/shard_map/ppermute | solution.py:375
  24.4 1.3 collective-permute-start.3
  25.7 2.0 %collective-permute-done.5 = bf16[2,128,128]{2,1,0:T(8,128)(2,1)S(1)} collective-permute-done((bf16[2,128,128]{2,1,0:T(8,128)(2,1)S(1)}, bf16[2,128,128]{2,1,0:T(8,128)(2,1)S(1)}, u32[]{:S(2)}, u32[]{:S(2)}) %collective-permute-start.5) | collective-permute-done | bytes 65568 | tf_op jit(solution)/shard_map/ppermute | solution.py:375
  27.7 3.0 %collective-permute-done.4 = bf16[2,128,128]{2,1,0:T(8,128)(2,1)S(1)} collective-permute-done((bf16[2,128,128]{2,1,0:T(8,128)(2,1)S(1)}, bf16[2,128,128]{2,1,0:T(8,128)(2,1)S(1)}, u32[]{:S(2)}, u32[]{:S(2)}) %collective-permute-start.4) | collective-permute-done | bytes 65568 | tf_op jit(solution)/shard_map/ppermute | solution.py:375
  31.9 3.1 %collective-permute-start = (bf16[128,4096]{1,0:T(8,128)(2,1)S(1)}, bf16[128,4096]{1,0:T(8,128)(2,1)S(1)}, u32[]{:S(2)}, u32[]{:S(2)}) collective-permute-start(bf16[128,4096]{1,0:T(8,128)(2,1)S(1)} %copy-done.1), channel_id=1, source_target_pairs={{0,18},{1,19},{2,16},{3,17},{4,22},{5,23},{6,20},{7,21},{8,26},{9,... | collective-permute-start | bytes 3145736 | tf_op jit(solution)/shard_map/ppermute | solution.py:363
  35.9 6.2 %project_q.2 = bf16[2,8,128,128]{3,2,1,0:T(8,128)(2,1)S(1)} custom-call(bf16[128,4096]{1,0:T(8,128)(2,1)S(1)} %copy-done.1, bf16[128,4096]{1,0:T(8,128)(2,1)S(1)} %collective-permute-done.1.x1, bf16[256,64]{1,0:T(8,128)(2,1)S(1)} %get-tuple-element.11.mid, bf16[4096,1536]{1,0:T(8,128)(2,1)} %w.7, bf16[64,1536]{1,0:T(8,128)(2,1)S(1)} %copy-done.5, ...), custom_call_target="tpu_custom_call" | custom-call | flops 2147483648 | bytes 8388608 | tf_op jit(solution)/shard_map/project_q/pallas_call | solution.py:147
  42.1 16.0 %collective-permute-done.x0 = bf16[128,4096]{1,0:T(8,128)(2,1)S(1)} collective-permute-done((bf16[128,4096]{1,0:T(8,128)(2,1)S(1)}, bf16[128,4096]{1,0:T(8,128)(2,1)S(1)}, u32[]{:S(2)}, u32[]{:S(2)}) %collective-permute-start) | collective-permute-done | bytes 1048608 | tf_op jit(solution)/shard_map/ppermute | solution.py:363
  58.3 2.5 %collective-permute-done.7.x1 = bf16[128,4096]{1,0:T(8,128)(2,1)S(1)} collective-permute-done((bf16[128,4096]{1,0:T(8,128)(2,1)S(1)}, bf16[128,4096]{1,0:T(8,128)(2,1)S(1)}, u32[]{:S(2)}, u32[]{:S(2)}) %collective-permute-start.7) | collective-permute-done | bytes 1048608 | tf_op jit(solution)/shard_map/ppermute | solution.py:387
  60.9 4.0 %project_kv.3 = (bf16[2,2,2,128,128]{4,3,2,1,0:T(8,128)(2,1)S(1)}, bf16[256,64]{1,0:T(8,128)(2,1)S(1)}) custom-call(bf16[128,4096]{1,0:T(8,128)(2,1)S(1)} %collective-permute-done.x0, bf16[128,4096]{1,0:T(8,128)(2,1)S(1)} %collective-permute-done.7.x1, bf16[4096,1536]{1,0:T(8,128)(2,1)} %w.7, bf16[4096,64]{1,0:T(8,128)(2,1)S(1)} %copy.11.down, ...), custom_call_target="tpu_custom_call" | custom-call | flops 1073741824 | bytes 4194304 | tf_op jit(solution)/shard_map/project_kv/pallas_call | solution.py:115
  68.6 2.8 %collective-permute-done.13 = bf16[2,128,128]{2,1,0:T(8,128)(2,1)S(1)} collective-permute-done((bf16[2,128,128]{2,1,0:T(8,128)(2,1)S(1)}, bf16[2,128,128]{2,1,0:T(8,128)(2,1)S(1)}, u32[]{:S(2)}, u32[]{:S(2)}) %collective-permute-start.13) | collective-permute-done | bytes 65568 | tf_op jit(solution)/shard_map/ppermute | solution.py:375
  77.1 6.0 %project_q.3 = bf16[2,8,128,128]{3,2,1,0:T(8,128)(2,1)S(1)} custom-call(bf16[128,4096]{1,0:T(8,128)(2,1)S(1)} %copy-done.3, bf16[128,4096]{1,0:T(8,128)(2,1)S(1)} %collective-permute-done.7.x1, bf16[256,64]{1,0:T(8,128)(2,1)S(1)} %get-tuple-element.15.mid, bf16[4096,1536]{1,0:T(8,128)(2,1)} %w.7, bf16[64,1536]{1,0:T(8,128)(2,1)S(1)} %copy-done.5, ...), custom_call_target="tpu_custom_call" | custom-call | flops 2147483648 | bytes 8388608 | tf_op jit(solution)/shard_map/project_q/pallas_call | solution.py:147
  83.2 2.9 %collective-permute-start.8 = (bf16[8,128,128]{2,1,0:T(8,128)(2,1)S(1)}, bf16[8,128,128]{2,1,0:T(8,128)(2,1)S(1)}, u32[]{:S(2)}, u32[]{:S(2)}) collective-permute-start(bf16[8,128,128]{2,1,0:T(8,128)(2,1)S(1)} %get-tuple-element.18), channel_id=1, source_target_pairs={{0,18},{1,19},{2,16},{3,17},{4,22},{5,23},{6,20},{7,21},{8,26},{9,... | collective-permute-start | bytes 786440 | tf_op jit(solution)/shard_map/ppermute | solution.py:395
  86.5 7.1 %collective-permute-done.8.c = bf16[8,128,128]{2,1,0:T(8,128)(2,1)S(1)} collective-permute-done((bf16[8,128,128]{2,1,0:T(8,128)(2,1)S(1)}, bf16[8,128,128]{2,1,0:T(8,128)(2,1)S(1)}, u32[]{:S(2)}, u32[]{:S(2)}) %collective-permute-start.8) | collective-permute-done | bytes 262176 | tf_op jit(solution)/shard_map/ppermute | solution.py:395
  93.6 4.8 %collective-permute-done.9.d = bf16[8,128,128]{2,1,0:T(8,128)(2,1)S(1)} collective-permute-done((bf16[8,128,128]{2,1,0:T(8,128)(2,1)S(1)}, bf16[8,128,128]{2,1,0:T(8,128)(2,1)S(1)}, u32[]{:S(2)}, u32[]{:S(2)}) %collective-permute-start.9) | collective-permute-done | bytes 262176 | tf_op jit(solution)/shard_map/ppermute | solution.py:396
  98.4 2.5 %sort_heads.1 = bf16[8,4,128,128]{3,2,1,0:T(8,128)(2,1)} custom-call(s32[32]{0:T(128)S(1)} %select_reduce_fusion.source, bf16[8,128,128]{2,1,0:T(8,128)(2,1)S(1)} %get-tuple-element.20.a, bf16[8,128,128]{2,1,0:T(8,128)(2,1)S(1)} %collective-permute-done.6.b, bf16[8,128,128]{2,1,0:T(8,128)(2,1)S(1)} %collective-permute-done.8.c, ...), custom_call_target="tpu_custom_call" | custom-call | bytes 2097152 | tf_op jit(solution)/shard_map/sort_heads/pallas_call | solution.py:183
  100.9 7.8 %all-to-all-start = ((bf16[8,4,128,128]{3,2,1,0:T(8,128)(2,1)}), bf16[8,4,128,128]{3,2,1,0:T(8,128)(2,1)S(1)}, u32[]{:S(2)}, u32[]{:S(2)}) async-start(bf16[8,4,128,128]{3,2,1,0:T(8,128)(2,1)} %sort_heads.1), calls=%async_computation | async-start | bytes 2097152 | tf_op jit(solution)/shard_map/all_to_all | solution.py:405
  110.7 18.0 %all-to-all-done.q_ref = bf16[8,4,128,128]{3,2,1,0:T(8,128)(2,1)S(1)} async-done(((bf16[8,4,128,128]{3,2,1,0:T(8,128)(2,1)}), bf16[8,4,128,128]{3,2,1,0:T(8,128)(2,1)S(1)}, u32[]{:S(2)}, u32[]{:S(2)}) %all-to-all-start) | async-done | bytes 1048608 | tf_op jit(solution)/shard_map/all_to_all | solution.py:405
  129.6 31.9 %attend.1 = bf16[8,4,128,128]{3,2,1,0:T(8,128)(2,1)} custom-call(s32[8]{0:T(128)} %multiply_add_fusion.blocks, s32[4]{0:T(128)} %convert_reduce_fusion.starts, s32[2]{0:T(128)} %pad_add_fusion.own, bf16[8,4,128,128]{3,2,1,0:T(8,128)(2,1)} %copy-done.9, bf16[16,4,2,128,128]{4,3,2,1,0:T(8,128)(2,1)} %bitcast.52, bf16[16,4,2,128,128]{4,3,2,1,0:T(8,128)(2,1)} %bitcast.53), custom_call_target="tpu_custom_call" | custom-call | flops 10000000000 | bytes 10485760 | tf_op jit(solution)/shard_map/attend/pallas_call | solution.py:333
  161.5 24.6 %all_to_all.10.a = bf16[8,4,128,128]{3,2,1,0:T(8,128)(2,1)S(1)} all-to-all(bf16[8,4,128,128]{3,2,1,0:T(8,128)(2,1)} %attend.1), channel_id=1, replica_groups={{0,18,36,54,72,90,108,126},{1,19,37,55,73,91,109,127},{16,2,52,38,88,74..., dimensions={0} | all-to-all | bytes 2097152 | tf_op jit(solution)/shard_map/all_to_all | solution.py:414
  186.1 1.9 unsort_heads.1
  (78 shorter events, 19.9 us)
Async XLA Ops:
  6.5 122.1 %all-gather.5.cloned.1.call-start = ((), (), s32[]{:S(2)}) async-start(), calls=%async_computation.2 | async-start | bytes 4456448 | tf_op jit(solution)/shard_map/all_gather | solution.py:379
  6.5 3.7 %collective-permute-start.1 = (bf16[128,4096]{1,0:T(8,128)(2,1)}, bf16[128,4096]{1,0:T(8,128)(2,1)S(1)}, u32[]{:S(2)}, u32[]{:S(2)}) collective-permute-start(bf16[128,4096]{1,0:T(8,128)(2,1)} %x0.3), channel_id=1, source_target_pairs={{0,1},{1,0},{2,3},{3,2},{4,5},{5,4},{6,7},{7,6},{8,9},{9,8},{10,11... | collective-permute-start | bytes 3145736 | tf_op jit(solution)/shard_map/ppermute | solution.py:364
  12.4 19.5 %copy-start.1 = (bf16[128,4096]{1,0:T(8,128)(2,1)S(1)}, bf16[128,4096]{1,0:T(8,128)(2,1)}, u32[]{:S(2)}) copy-start(bf16[128,4096]{1,0:T(8,128)(2,1)} %x0.3) | copy-start | bytes 3145732
  12.4 22.6 %copy-start.5 = (bf16[64,1536]{1,0:T(8,128)(2,1)S(1)}, bf16[64,1536]{1,0:T(8,128)(2,1)}, u32[]{:S(2)}) copy-start(bf16[64,1536]{1,0:T(8,128)(2,1)} %up.7) | copy-start | bytes 589828
  17.2 1.8 collective-permute-start.2
  20.2 7.5 %collective-permute-start.5 = (bf16[2,128,128]{2,1,0:T(8,128)(2,1)S(1)}, bf16[2,128,128]{2,1,0:T(8,128)(2,1)S(1)}, u32[]{:S(2)}, u32[]{:S(2)}) collective-permute-start(bf16[2,128,128]{2,1,0:T(8,128)(2,1)S(1)} %get-tuple-element.28), channel_id=1, source_target_pairs={{0,96},{32,0},{64,32},{96,64},{1,97},{33,1},{65,33},{97,65},{2,98}... | collective-permute-start | bytes 196616 | tf_op jit(solution)/shard_map/ppermute | solution.py:375
  24.4 6.3 %collective-permute-start.4 = (bf16[2,128,128]{2,1,0:T(8,128)(2,1)S(1)}, bf16[2,128,128]{2,1,0:T(8,128)(2,1)S(1)}, u32[]{:S(2)}, u32[]{:S(2)}) collective-permute-start(bf16[2,128,128]{2,1,0:T(8,128)(2,1)S(1)} %get-tuple-element.29), channel_id=1, source_target_pairs={{0,64},{32,96},{64,0},{96,32},{1,65},{33,97},{65,1},{97,33},{2,66}... | collective-permute-start | bytes 196616 | tf_op jit(solution)/shard_map/ppermute | solution.py:375
  24.4 6.7 %collective-permute-start.3 = (bf16[2,128,128]{2,1,0:T(8,128)(2,1)S(1)}, bf16[2,128,128]{2,1,0:T(8,128)(2,1)S(1)}, u32[]{:S(2)}, u32[]{:S(2)}) collective-permute-start(bf16[2,128,128]{2,1,0:T(8,128)(2,1)S(1)} %get-tuple-element.30), channel_id=1, source_target_pairs={{0,32},{32,64},{64,96},{96,0},{1,33},{33,65},{65,97},{97,1},{2,34}... | collective-permute-start | bytes 196616 | tf_op jit(solution)/shard_map/ppermute | solution.py:375
  31.9 96.8 %all-gather.7.cloned.1.call-start = ((), (), s32[]{:S(2)}) async-start(), calls=%async_computation.3 | async-start | bytes 4456448 | tf_op jit(solution)/shard_map/all_gather | solution.py:379
  31.9 26.2 %collective-permute-start = (bf16[128,4096]{1,0:T(8,128)(2,1)S(1)}, bf16[128,4096]{1,0:T(8,128)(2,1)S(1)}, u32[]{:S(2)}, u32[]{:S(2)}) collective-permute-start(bf16[128,4096]{1,0:T(8,128)(2,1)S(1)} %copy-done.1), channel_id=1, source_target_pairs={{0,18},{1,19},{2,16},{3,17},{4,22},{5,23},{6,20},{7,21},{8,26},{9,... | collective-permute-start | bytes 3145736 | tf_op jit(solution)/shard_map/ppermute | solution.py:363
  35.9 22.2 %copy-start.12 = (f32[256,64]{1,0:T(8,128)S(1)}, f32[256,64]{1,0:T(8,128)}, u32[]{:S(2)}) copy-start(f32[256,64]{1,0:T(8,128)} %get-tuple-element.34) | copy-start | bytes 196612
  35.9 22.3 %copy-start.10 = (f32[256,64]{1,0:T(8,128)S(1)}, f32[256,64]{1,0:T(8,128)}, u32[]{:S(2)}) copy-start(f32[256,64]{1,0:T(8,128)} %get-tuple-element.33) | copy-start | bytes 196612
  35.9 22.3 %copy-start.11 = (f32[256,64]{1,0:T(8,128)S(1)}, f32[256,64]{1,0:T(8,128)}, u32[]{:S(2)}) copy-start(f32[256,64]{1,0:T(8,128)} %get-tuple-element.35) | copy-start | bytes 196612
  42.1 22.8 %copy-start.6 = (bf16[2,8,128,128]{3,2,1,0:T(8,128)(2,1)}, bf16[2,8,128,128]{3,2,1,0:T(8,128)(2,1)S(1)}, u32[]{:S(2)}) copy-start(bf16[2,8,128,128]{3,2,1,0:T(8,128)(2,1)S(1)} %project_q.2) | copy-start | bytes 1572868
  58.1 2.8 %collective-permute-start.7 = (bf16[128,4096]{1,0:T(8,128)(2,1)S(1)}, bf16[128,4096]{1,0:T(8,128)(2,1)S(1)}, u32[]{:S(2)}, u32[]{:S(2)}) collective-permute-start(bf16[128,4096]{1,0:T(8,128)(2,1)S(1)} %collective-permute-done.x0), channel_id=1, source_target_pairs={{0,1},{1,0},{2,3},{3,2},{4,5},{5,4},{6,7},{7,6},{8,9},{9,8},{10,11... | collective-permute-start | bytes 3145736 | tf_op jit(solution)/shard_map/ppermute | solution.py:387
  65.0 1.4 collective-permute-start.10
  66.5 4.9 %collective-permute-start.13 = (bf16[2,128,128]{2,1,0:T(8,128)(2,1)S(1)}, bf16[2,128,128]{2,1,0:T(8,128)(2,1)S(1)}, u32[]{:S(2)}, u32[]{:S(2)}) collective-permute-start(bf16[2,128,128]{2,1,0:T(8,128)(2,1)S(1)} %get-tuple-element.22), channel_id=1, source_target_pairs={{0,96},{32,0},{64,32},{96,64},{1,97},{33,1},{65,33},{97,65},{2,98}... | collective-permute-start | bytes 196616 | tf_op jit(solution)/shard_map/ppermute | solution.py:375
  66.7 5.9 %collective-permute-start.12 = (bf16[2,128,128]{2,1,0:T(8,128)(2,1)S(1)}, bf16[2,128,128]{2,1,0:T(8,128)(2,1)S(1)}, u32[]{:S(2)}, u32[]{:S(2)}) collective-permute-start(bf16[2,128,128]{2,1,0:T(8,128)(2,1)S(1)} %get-tuple-element.23), channel_id=1, source_target_pairs={{0,64},{32,96},{64,0},{96,32},{1,65},{33,97},{65,1},{97,33},{2,66}... | collective-permute-start | bytes 196616 | tf_op jit(solution)/shard_map/ppermute | solution.py:375
  67.3 6.5 %collective-permute-start.11 = (bf16[2,128,128]{2,1,0:T(8,128)(2,1)S(1)}, bf16[2,128,128]{2,1,0:T(8,128)(2,1)S(1)}, u32[]{:S(2)}, u32[]{:S(2)}) collective-permute-start(bf16[2,128,128]{2,1,0:T(8,128)(2,1)S(1)} %get-tuple-element.24), channel_id=1, source_target_pairs={{0,32},{32,64},{64,96},{96,0},{1,33},{33,65},{65,97},{97,1},{2,34}... | collective-permute-start | bytes 196616 | tf_op jit(solution)/shard_map/ppermute | solution.py:375
  75.8 10.7 %collective-permute-start.6 = (bf16[8,128,128]{2,1,0:T(8,128)(2,1)S(1)}, bf16[8,128,128]{2,1,0:T(8,128)(2,1)S(1)}, u32[]{:S(2)}, u32[]{:S(2)}) collective-permute-start(bf16[8,128,128]{2,1,0:T(8,128)(2,1)S(1)} %get-tuple-element.19), channel_id=1, source_target_pairs={{0,1},{1,0},{2,3},{3,2},{4,5},{5,4},{6,7},{7,6},{8,9},{9,8},{10,11... | collective-permute-start | bytes 786440 | tf_op jit(solution)/shard_map/ppermute | solution.py:394
  83.1 26.7 %copy-start.13 = (s32[16384]{0:T(1024)S(1)}, s32[16384]{0:T(1024)}, u32[]{:S(2)}) copy-start(s32[16384]{0:T(1024)} %param.10) | copy-start | bytes 196612
  83.2 10.4 %collective-permute-start.8 = (bf16[8,128,128]{2,1,0:T(8,128)(2,1)S(1)}, bf16[8,128,128]{2,1,0:T(8,128)(2,1)S(1)}, u32[]{:S(2)}, u32[]{:S(2)}) collective-permute-start(bf16[8,128,128]{2,1,0:T(8,128)(2,1)S(1)} %get-tuple-element.18), channel_id=1, source_target_pairs={{0,18},{1,19},{2,16},{3,17},{4,22},{5,23},{6,20},{7,21},{8,26},{9,... | collective-permute-start | bytes 786440 | tf_op jit(solution)/shard_map/ppermute | solution.py:395
  86.1 12.3 %collective-permute-start.9 = (bf16[8,128,128]{2,1,0:T(8,128)(2,1)S(1)}, bf16[8,128,128]{2,1,0:T(8,128)(2,1)S(1)}, u32[]{:S(2)}, u32[]{:S(2)}) collective-permute-start(bf16[8,128,128]{2,1,0:T(8,128)(2,1)S(1)} %get-tuple-element.17), channel_id=1, source_target_pairs={{0,19},{1,18},{2,17},{3,16},{4,23},{5,22},{6,21},{7,20},{8,27},{9,... | collective-permute-start | bytes 786440 | tf_op jit(solution)/shard_map/ppermute | solution.py:396
  100.9 27.7 %all-to-all-start = ((bf16[8,4,128,128]{3,2,1,0:T(8,128)(2,1)}), bf16[8,4,128,128]{3,2,1,0:T(8,128)(2,1)S(1)}, u32[]{:S(2)}, u32[]{:S(2)}) async-start(bf16[8,4,128,128]{3,2,1,0:T(8,128)(2,1)} %sort_heads.1), calls=%async_computation | async-start | bytes 2097152 | tf_op jit(solution)/shard_map/all_to_all | solution.py:405
  (8 other events, 34.7 us)
Sparse Core Ops, SparseCore 0:
  32.0 36.7 all-gather.4
  74.7 38.3 all-gather.6

commit v3 on v2

--- a/solution.py
+++ b/solution.py
@@ -61,15 +61,23 @@
     return part * cosine + pltpu.roll(part, DH // 2, 1) * sine
 
 
-def kv_kernel(x0, x1, w, down, up, cosine, sine, out, mid_out, rows, mid):
+def gather_rows(x0, x1, rows):
+    rows[:BLK] = x0[...]
+    rows[BLK:] = x1[...]
+
+
+def kv_kernel(makes_mid, x0, x1, w, low, up, cosine, sine, out, *rest):
     step = pl.program_id(0)
+    if makes_mid:
+        mid, rows = rest
+    else:
+        mid, (rows,) = low, rest
 
     @pl.when(step == 0)
     def _():
-        rows[:BLK] = x0[...]
-        rows[BLK:] = x1[...]
-        mid[...] = jnp.dot(rows[...], down[...], preferred_element_type=F32).astype(BF)
-        mid_out[...] = mid[...]
+        gather_rows(x0, x1, rows)
+        if makes_mid:
+            mid[...] = jnp.dot(rows[...], low[...], preferred_element_type=F32).astype(BF)
 
     acc = jnp.dot(rows[...], w[...], preferred_element_type=F32)
     acc = acc + ADAPTER_SCALE * jnp.dot(mid[...], up[...], preferred_element_type=F32)
@@ -89,13 +97,18 @@
                 out[block, head, 0] = part[block * BLK:(block + 1) * BLK]
 
 
-def q_kernel(x0, x1, mid, w, up, cosine, sine, out, rows):
+def q_kernel(makes_mid, x0, x1, w, low, up, cosine, sine, out, *rest):
     step = pl.program_id(0)
+    if makes_mid:
+        mid, rows = rest
+    else:
+        mid, (rows,) = low, rest
 
     @pl.when(step == 0)
     def _():
-        rows[:BLK] = x0[...]
-        rows[BLK:] = x1[...]
+        gather_rows(x0, x1, rows)
+        if makes_mid:
+            mid[...] = jnp.dot(rows[...], low[...], preferred_element_type=F32).astype(BF)
 
     acc = jnp.dot(rows[...], w[...], preferred_element_type=F32)
     acc = acc + ADAPTER_SCALE * jnp.dot(mid[...], up[...], preferred_element_type=F32)
@@ -105,66 +118,111 @@
             out[block, head] = part[block * BLK:(block + 1) * BLK]
 
 
-def whole(shape):
-    return pl.BlockSpec(shape, lambda *_: (0,) * len(shape))
-
-
-def project_kv(x0, x1, w, down, up, cosine, sine):
+def both_kernel(x0, x1, w, low, up, cosine, sine, out_q, out_kv, mid, rows):
+    step = pl.program_id(0)
+
+    @pl.when(step == 0)
+    def _():
+        gather_rows(x0, x1, rows)
+        mid[...] = jnp.dot(rows[...], low[...], preferred_element_type=F32).astype(BF)
+
+    acc = jnp.dot(rows[...], w[...], preferred_element_type=F32)
+    acc = acc + ADAPTER_SCALE * jnp.dot(mid[...], up[...], preferred_element_type=F32)
+
+    @pl.when(step < 4)
+    def _():
+        for head in range(2):
+            part = rotated(acc[:, head * DH:(head + 1) * DH], cosine[...], sine[...]).astype(BF)
+            for block in range(2):
+                out_q[block, head] = part[block * BLK:(block + 1) * BLK]
+
+    @pl.when(step == 4)
+    def _():
+        for head in range(2):
+            part = rotated(acc[:, head * DH:(head + 1) * DH], cosine[...], sine[...]).astype(BF)
+            for block in range(2):
+                out_kv[block, head, 0] = part[block * BLK:(block + 1) * BLK]
+
+    @pl.when(step == 5)
+    def _():
+        for head in range(2):
+            part = acc[:, head * DH:(head + 1) * DH].astype(BF)
+            for block in range(2):
+                out_kv[block, head, 0] = part[block * BLK:(block + 1) * BLK]
+
+
+def project_both(x0, x1, w, down, up, cosine, sine):
     width = x0.shape[1]
     rank = down.shape[1]
     return pl.pallas_call(
-        kv_kernel,
-        grid=(2,),
+        both_kernel,
+        grid=(6,),
         in_specs=[
             whole((BLK, width)),
             whole((BLK, width)),
-            pl.BlockSpec((width, 2 * DH), lambda j: (0, 4 + j)),
-            whole((width, rank)),
-            pl.BlockSpec((rank, 2 * DH), lambda j: (0, 4 + j)),
+            pl.BlockSpec((width, 2 * DH), lambda j: (0, j)),
+            whole(down.shape),
+            pl.BlockSpec((rank, 2 * DH), lambda j: (0, j)),
             whole((2 * BLK, DH)),
             whole((2 * BLK, DH)),
         ],
         out_specs=[
-            pl.BlockSpec((2, 2, 1, BLK, DH), lambda j: (0, 0, j, 0, 0)),
-            whole((2 * BLK, rank)),
+            pl.BlockSpec((2, 2, BLK, DH), lambda j: (0, jnp.minimum(j, 3), 0, 0)),
+            pl.BlockSpec((2, 2, 1, BLK, DH), lambda j: (0, 0, jnp.maximum(j - 4, 0), 0, 0)),
         ],
         out_shape=[
+            jax.ShapeDtypeStruct((2, 8, BLK, DH), BF),
             jax.ShapeDtypeStruct((2, 2, 2, BLK, DH), BF),
-            jax.ShapeDtypeStruct((2 * BLK, rank), BF),
-        ],
-        scratch_shapes=[pltpu.VMEM((2 * BLK, width), BF), pltpu.VMEM((2 * BLK, rank), BF)],
+        ],
+        scratch_shapes=[pltpu.VMEM((2 * BLK, rank), BF), pltpu.VMEM((2 * BLK, width), BF)],
         compiler_params=pltpu.CompilerParams(vmem_limit_bytes=40 * 2**20),
         cost_estimate=pl.CostEstimate(
-            flops=2 * 2 * BLK * width * 4 * DH, bytes_accessed=width * 4 * DH * 2, transcendentals=0
+            flops=2 * 2 * BLK * width * 12 * DH, bytes_accessed=width * 12 * DH * 2, transcendentals=0
         ),
-        name="project_kv",
+        name="project_both",
     )(x0, x1, w, down, up, cosine, sine)
 
 
-def project_q(x0, x1, mid, w, up, cosine, sine):
+def whole(shape):
+    return pl.BlockSpec(shape, lambda *_: (0,) * len(shape))
+
+
+def project(for_keys, x0, x1, w, low, up, cosine, sine):
     width = x0.shape[1]
-    rank = mid.shape[1]
-    return pl.pallas_call(
-        q_kernel,
-        grid=(4,),
+    rank = low.shape[1]
+    makes_mid = low.shape[0] == width
+    steps, base = (2, 4) if for_keys else (4, 0)
+    if for_keys:
+        out_spec = pl.BlockSpec((2, 2, 1, BLK, DH), lambda j: (0, 0, j, 0, 0))
+        out_shape = jax.ShapeDtypeStruct((2, 2, 2, BLK, DH), BF)
+    else:
+        out_spec = pl.BlockSpec((2, 2, BLK, DH), lambda j: (0, j, 0, 0))
+        out_shape = jax.ShapeDtypeStruct((2, 8, BLK, DH), BF)
+    mid_spec, mid_shape = [], []
+    if makes_mid:
+        mid_spec, mid_shape = [whole((2 * BLK, rank))], [jax.ShapeDtypeStruct((2 * BLK, rank), BF)]
+    made = pl.pallas_call(
+        functools.partial(kv_kernel if for_keys else q_kernel, makes_mid),
+        grid=(steps,),
         in_specs=[
             whole((BLK, width)),
             whole((BLK, width)),
-            whole((2 * BLK, rank)),
-            pl.BlockSpec((width, 2 * DH), lambda j: (0, j)),
-            pl.BlockSpec((rank, 2 * DH), lambda j: (0, j)),
+            pl.BlockSpec((width, 2 * DH), lambda j: (0, base + j)),
+            whole(low.shape),
+            pl.BlockSpec((rank, 2 * DH), lambda j: (0, base + j)),
             whole((2 * BLK, DH)),
             whole((2 * BLK, DH)),
         ],
-        out_specs=pl.BlockSpec((2, 2, BLK, DH), lambda j: (0, j, 0, 0)),
-        out_shape=jax.ShapeDtypeStruct((2, 8, BLK, DH), BF),
+        out_specs=[out_spec] + mid_spec,
+        out_shape=[out_shape] + mid_shape,
         scratch_shapes=[pltpu.VMEM((2 * BLK, width), BF)],
         compiler_params=pltpu.CompilerParams(vmem_limit_bytes=40 * 2**20),
         cost_estimate=pl.CostEstimate(
-            flops=2 * 2 * BLK * width * 8 * DH, bytes_accessed=width * 8 * DH * 2, transcendentals=0
+            flops=2 * 2 * BLK * width * 2 * DH * steps, bytes_accessed=width * 2 * DH * steps * 2, transcendentals=0
         ),
-        name="project_q",
-    )(x0, x1, mid, w, up, cosine, sine)
+        name="project_kv" if for_keys else "project_q",
+    )(x0, x1, w, low, up, cosine, sine)
+    return made if makes_mid else made[0]
 
 
 def sort_kernel(source, a, b, c, d, out):
@@ -209,18 +267,16 @@
     )(slots, a)
 
 
-def attend_kernel(blocks, starts, own, q_ref, kv0, kv1, out, pairs, sems, top, total, acc, floor):
+def attend_kernel(blocks, starts, own, q_ref, kv, out, pairs, sems, top, total, acc, floor):
     yh = own[0]
 
-    def copies_of(z):
-        return [
-            pltpu.make_async_copy(src.at[:, pl.ds((own[1] - z + NZ) % NZ, 1)], pairs.at[stage, :, pl.ds(z, 1)], sems.at[2 * z + stage])
-            for stage, src in enumerate((kv0, kv1))
-        ]
+    def copy_of(z):
+        return pltpu.make_async_copy(
+            kv.at[:, pl.ds((own[1] - z + NZ) % NZ, 1)], pairs.at[:, pl.ds(z, 1)], sems.at[z]
+        )
 
     for z in range(NZ):
-        for copy in copies_of(z):
-            copy.start()
+        copy_of(z).start()
 
     def gathered(begin_block, width, kind):
         parts = []
@@ -229,7 +285,7 @@
             low = (key_block // (NC * NYH * NX)) % NYL
             stage = ((key_block // NC) % NYH) ^ yh
             source = (((key_block // (NC * NYH)) % NX) * NYL + (low ^ stage)) * NC + key_block % NC
-            parts.append(pairs[stage, source, key_block // (NC * NYH * NX * NYL), kind])
+            parts.append(pairs[source, key_block // (NC * NYH * NX * NYL), stage, kind])
         return jnp.concatenate(parts, axis=0)
 
     def one_tile(tile):
@@ -319,8 +375,7 @@
         out[tile] = (acc[...] / jnp.sum(total[...], axis=1, keepdims=True)).astype(BF).reshape(4, BLK, DH)
 
     def pair(z, carry):
-        for copy in copies_of(z):
-            copy.wait()
+        copy_of(z).wait()
         one_tile(2 * z)
         one_tile(2 * z + 1)
         return carry
@@ -328,7 +383,7 @@
     lax.fori_loop(0, NZ, pair, 0)
 
 
-def attend(blocks, starts, own, q, kv0, kv1):
+def attend(blocks, starts, own, q, kv):
     rows = 4 * BLK
     return pl.pallas_call(
         attend_kernel,
@@ -336,13 +391,12 @@
         + [
             pl.BlockSpec(memory_space=pltpu.VMEM),
             pl.BlockSpec(memory_space=pl.ANY),
-            pl.BlockSpec(memory_space=pl.ANY),
         ],
         out_specs=pl.BlockSpec(memory_space=pltpu.VMEM),
         out_shape=jax.ShapeDtypeStruct((8, 4, BLK, DH), BF),
         scratch_shapes=[
-            pltpu.VMEM((2, NX * NYL * NC, NZ, 2, BLK, DH), BF),
-            pltpu.SemaphoreType.DMA((2 * NZ,)),
+            pltpu.VMEM((NX * NYL * NC, NZ, 2, 2, BLK, DH), BF),
+            pltpu.SemaphoreType.DMA((NZ,)),
             pltpu.VMEM((rows, DH), F32),
             pltpu.VMEM((rows, DH), F32),
             pltpu.VMEM((rows, DH), F32),
@@ -351,7 +405,7 @@
         compiler_params=pltpu.CompilerParams(vmem_limit_bytes=60 * 2**20),
         cost_estimate=pl.CostEstimate(flops=10**10, bytes_accessed=10 * 2**20, transcendentals=10**7),
         name="attend",
-    )(blocks, starts, own, q, kv0, kv1)
+    )(blocks, starts, own, q, kv)
 
 
 def per_device(tokens, w, down, up, document_index, query_to_key_head):
@@ -366,8 +420,8 @@
     near_cos, near_sin = rope_tables(jnp.stack([block, block + other]))
     far_cos, far_sin = rope_tables(jnp.stack([far_block, far_block + other]))
 
-    def split_kv(kv):
-        mine, theirs = kv[0], lax.ppermute(kv[1], "c", SWAP)
+    def split_kv(near, far):
+        mine, theirs = jnp.stack([near[0], far[0]], 1), lax.ppermute(jnp.stack([near[1], far[1]], 1), "c", SWAP)
         heads = jnp.where(c == 0, jnp.concatenate([mine, theirs], 0), jnp.concatenate([theirs, mine], 0))
         rows = []
         for k in range(NZ):
@@ -375,25 +429,22 @@
             rows.append(lax.ppermute(head, "z", [(i, (i + k) % NZ) for i in range(NZ)]) if k else head)
         return jnp.stack(rows)[None]
 
-    def spread_kv(rows):
-        return lax.all_gather(rows, ("x", "yl", "c"), axis=0, tiled=True)
-
-    kv_near, mid_near = project_kv(tokens, near_pair, w, down, up, near_cos, near_sin)
-    rows_near = split_kv(kv_near)
-    kv0 = spread_kv(rows_near)
-    q_near = project_q(tokens, near_pair, mid_near, w, up, near_cos, near_sin)
-
-    far, q_near, rows_near = lax.optimization_barrier((far, q_near, rows_near))
+    q_near, kv_near = project_both(tokens, near_pair, w, down, up, near_cos, near_sin)
+    far, q_near, kv_near = lax.optimization_barrier((far, q_near, kv_near))
     far_pair = lax.ppermute(far, "c", SWAP)
-    kv_far, mid_far = project_kv(far, far_pair, w, down, up, far_cos, far_sin)
-    kv1 = spread_kv(split_kv(kv_far))
-    q_far = project_q(far, far_pair, mid_far, w, up, far_cos, far_sin)
+    q_far, mid_far = project(False, far, far_pair, w, down, up, far_cos, far_sin)
+    home_c = lax.ppermute(q_far[0], ALL, CROSS)
+    home_d = lax.ppermute(q_far[1], ALL, CROSS_OTHER)
+    kv_far = project(True, far, far_pair, w, mid_far, up, far_cos, far_sin)
+    kv_far, home_c = lax.optimization_barrier((kv_far, home_c))
+    rows, home_d = lax.optimization_barrier((split_kv(kv_near, kv_far), home_d))
+    kv = lax.all_gather(rows, ("x", "yl", "c"), axis=0, tiled=True)
 
     parts = (
         q_near[0],
         lax.ppermute(q_near[1], "c", SWAP),
-        lax.ppermute(q_far[0], ALL, CROSS),
-        lax.ppermute(q_far[1], ALL, CROSS_OTHER),
+        home_c,
+        home_d,
     )
     member = (query_to_key_head % 4) * 2 + query_to_key_head // 4
     heads = jnp.arange(H, dtype=jnp.int32)
@@ -410,7 +461,7 @@
     starts = jnp.sum(
         (document_index[None, :] < jnp.arange(DOCS, dtype=jnp.int32)[:, None]).astype(jnp.int32), axis=1
     )
-    context = attend(blocks, starts, jnp.stack([yh, z]).astype(jnp.int32), q, kv0, kv1)
+    context = attend(blocks, starts, jnp.stack([yh, z]).astype(jnp.int32), q, kv)
     home = lax.all_to_all(context, ALL, split_axis=0, concat_axis=0, tiled=True, axis_index_groups=GROUPS)
     return unsort_heads(slots, home)
 

time: 195 us -> 204 us (1.046); the launches traced: 195 us -> 200 us
  waiting for transfers between devices: 61.6 us -> 72.6 us
  local copies, waits for them, and re-layouts: 8.71 us -> 5.54 us
  other arithmetic: 7.13 us -> 4.01 us
  starting transfers between devices: 22.5 us -> 19.9 us
  blocking collectives: 24.6 us -> 26.7 us
    all_gather x2 -> x1, waiting for transfers between devices: 0.01 us -> 21.7 us  [per_device(): kv = lax.all_gather(rows, ('x', 'yl', 'c'), axis=0, tiled=True)]
    ppermute x5 -> x4, waiting for transfers between devices: 14.4 us -> 4.49 us  [the longest x1 3.12 us: per_device(): home_c = lax.ppermute(q_far[0], ALL, CROSS)]
    all_to_all x1, waiting for transfers between devices: 18 us -> 27.8 us  [per_device(): lax.all_to_all(sorted_q, ALL, split_axis=0, concat_axis=0, tiled=True, ax...]
    ppermute x1, waiting for transfers between devices: 16 us -> 8.12 us  [per_device(): far = lax.ppermute(tokens, ALL, CROSS)]
    all_to_all x1, starting transfers between devices: 7.84 us -> 5.21 us  [per_device(): lax.all_to_all(sorted_q, ALL, split_axis=0, concat_axis=0, tiled=True, ax...]
    ppermute x6 -> x3, waiting for transfers between devices: 10.6 us -> 8.03 us  [split_kv(): lax.ppermute(head, 'z', [(i, (i + k) % NZ) for i in range(NZ)])]
    unnamed x31 -> x15, local copies, waits for them, and re-layouts: 6.8 us -> 4.48 us
    ppermute x5 -> x4, starting transfers between devices: 3.94 us -> 6.19 us  [the longest x1 3.03 us: per_device(): home_c = lax.ppermute(q_far[0], ALL, CROSS)]
  transfers between devices with their start and end apart: 17 -> 12, of which waited for: 13 -> 9; matrix products, arithmetic and copies ran while one was open for 4% -> 3% of each run, Pallas kernels for 10% -> 8%
where the time goes in v3:
time: 204 us; the launch traced here: 200 us
  waiting for transfers between devices  72.6 us (36%)
  Pallas kernels  57.7 us (28%)
  blocking collectives  26.7 us (13%)
  starting transfers between devices  19.9 us (10%)
  between operations  13.7 us (7%)
  local copies, waits for them, and re-layouts  5.54 us (3%)
  other arithmetic  4.01 us (2%)
    pallas_call x1, Pallas kernels, attend(): pl.pallas_call(attend_kernel, in_specs=[pl.BlockSpec(memory_space=pltpu.S...  34.1 us
    all_to_all x1, waiting for transfers between devices, per_device(): lax.all_to_all(sorted_q, ALL, split_axis=0, concat_axis=0, tiled=True, ax...  27.8 us
    all_to_all x1, blocking collectives, per_device(): lax.all_to_all(context, ALL, split_axis=0, concat_axis=0, tiled=True, axi...  26.7 us
    all_gather x1, waiting for transfers between devices, per_device(): kv = lax.all_gather(rows, ('x', 'yl', 'c'), axis=0, tiled=True)  21.7 us
    pallas_call x2, Pallas kernels, project(): pl.pallas_call(functools.partial(kv_kernel if for_keys else q_kernel, mak...  10 us
    pallas_call x1, Pallas kernels, project_both(): pl.pallas_call(both_kernel, grid=(6,), in_specs=[whole((BLK, width)), who...  9.29 us
    ppermute x1, waiting for transfers between devices, per_device(): far = lax.ppermute(tokens, ALL, CROSS)  8.12 us
    ppermute x3, waiting for transfers between devices, split_kv(): lax.ppermute(head, 'z', [(i, (i + k) % NZ) for i in range(NZ)])  8.03 us
  transfers between devices with their start and end apart: 12, of which 9 were waited for; matrix products, arithmetic and copies ran while one was open for 3% of the time, Pallas kernels for 8%

profile of v3, /device:TPU:0, one launch (start us, length us, event | category | flops | bytes accessed | tf_op | source)
XLA Modules:
  0.0 200.2 jit_solution(15140584957589422330)
XLA Ops:
  6.5 3.1 %collective-permute-start = (bf16[128,4096]{1,0:T(8,128)(2,1)}, bf16[128,4096]{1,0:T(8,128)(2,1)S(1)}, u32[]{:S(2)}, u32[]{:S(2)}) collective-permute-start(bf16[128,4096]{1,0:T(8,128)(2,1)} %x0.1), channel_id=1, source_target_pairs={{0,18},{1,19},{2,16},{3,17},{4,22},{5,23},{6,20},{7,21},{8,26},{9,... | collective-permute-start | bytes 3145736 | tf_op jit(solution)/shard_map/ppermute | solution.py:417
  9.8 1.5 copy.12.low
  13.6 1.2 copy-done.1
  14.8 9.3 %project_both.1 = (bf16[2,8,128,128]{3,2,1,0:T(8,128)(2,1)S(1)}, bf16[2,2,2,128,128]{4,3,2,1,0:T(8,128)(2,1)S(1)}) custom-call(bf16[128,4096]{1,0:T(8,128)(2,1)S(1)} %copy-done.1, bf16[128,4096]{1,0:T(8,128)(2,1)S(1)} %collective-permute-done.1.x1, bf16[4096,1536]{1,0:T(8,128)(2,1)} %w.5, bf16[4096,64]{1,0:T(8,128)(2,1)S(1)} %copy.12.low, ...), custom_call_target="tpu_custom_call" | custom-call | flops 3221225472 | bytes 12582912 | tf_op jit(solution)/shard_map/project_both/pallas_call | solution.py:157
  24.9 8.1 %collective-permute-done.x0 = bf16[128,4096]{1,0:T(8,128)(2,1)S(1)} collective-permute-done((bf16[128,4096]{1,0:T(8,128)(2,1)}, bf16[128,4096]{1,0:T(8,128)(2,1)S(1)}, u32[]{:S(2)}, u32[]{:S(2)}) %collective-permute-start) | collective-permute-done | bytes 1048608 | tf_op jit(solution)/shard_map/ppermute | solution.py:417
  33.2 2.4 %collective-permute-done.3.x1 = bf16[128,4096]{1,0:T(8,128)(2,1)S(1)} collective-permute-done((bf16[128,4096]{1,0:T(8,128)(2,1)S(1)}, bf16[128,4096]{1,0:T(8,128)(2,1)S(1)}, u32[]{:S(2)}, u32[]{:S(2)}) %collective-permute-start.3) | collective-permute-done | bytes 1048608 | tf_op jit(solution)/shard_map/ppermute | solution.py:434
  35.7 6.6 %project_q.1 = (bf16[2,8,128,128]{3,2,1,0:T(8,128)(2,1)S(1)}, bf16[256,64]{1,0:T(8,128)(2,1)S(1)}) custom-call(bf16[128,4096]{1,0:T(8,128)(2,1)S(1)} %collective-permute-done.x0, bf16[128,4096]{1,0:T(8,128)(2,1)S(1)} %collective-permute-done.3.x1, bf16[4096,1536]{1,0:T(8,128)(2,1)} %w.5, bf16[4096,64]{1,0:T(8,128)(2,1)S(1)} %copy.12.low, ...), custom_call_target="tpu_custom_call" | custom-call | flops 2147483648 | bytes 8388608 | tf_op jit(solution)/shard_map/project_q/pallas_call | solution.py:204
  42.3 3.0 %collective-permute-start.4 = (bf16[8,128,128]{2,1,0:T(8,128)(2,1)S(1)}, bf16[8,128,128]{2,1,0:T(8,128)(2,1)S(1)}, u32[]{:S(2)}, u32[]{:S(2)}) collective-permute-start(bf16[8,128,128]{2,1,0:T(8,128)(2,1)S(1)} %get-tuple-element.28), channel_id=1, source_target_pairs={{0,18},{1,19},{2,16},{3,17},{4,22},{5,23},{6,20},{7,21},{8,26},{9,... | collective-permute-start | bytes 786440 | tf_op jit(solution)/shard_map/ppermute | solution.py:436
  45.4 3.5 %project_kv.1 = bf16[2,2,2,128,128]{4,3,2,1,0:T(8,128)(2,1)S(1)} custom-call(bf16[128,4096]{1,0:T(8,128)(2,1)S(1)} %collective-permute-done.x0, bf16[128,4096]{1,0:T(8,128)(2,1)S(1)} %collective-permute-done.3.x1, bf16[4096,1536]{1,0:T(8,128)(2,1)} %w.5, bf16[256,64]{1,0:T(8,128)(2,1)S(1)} %get-tuple-element.20.low, bf16[64,1536]{1,0:T(8,128)(2,1)S(1)} %copy-done, ...), custom_call_target="tpu_custom_call" | custom-call | flops 1073741824 | bytes 4194304 | tf_op jit(solution)/shard_map/project_kv/pallas_call | solution.py:204
  48.8 3.1 %collective-permute-done.4.c = bf16[8,128,128]{2,1,0:T(8,128)(2,1)S(1)} collective-permute-done((bf16[8,128,128]{2,1,0:T(8,128)(2,1)S(1)}, bf16[8,128,128]{2,1,0:T(8,128)(2,1)S(1)}, u32[]{:S(2)}, u32[]{:S(2)}) %collective-permute-start.4) | collective-permute-done | bytes 262176 | tf_op jit(solution)/shard_map/ppermute | solution.py:436
  52.2 3.0 %collective-permute-start.9 = (bf16[8,128,128]{2,1,0:T(8,128)(2,1)S(1)}, bf16[8,128,128]{2,1,0:T(8,128)(2,1)S(1)}, u32[]{:S(2)}, u32[]{:S(2)}) collective-permute-start(bf16[8,128,128]{2,1,0:T(8,128)(2,1)S(1)} %get-tuple-element.27), channel_id=1, source_target_pairs={{0,19},{1,18},{2,17},{3,16},{4,23},{5,22},{6,21},{7,20},{8,27},{9,... | collective-permute-start | bytes 786440 | tf_op jit(solution)/shard_map/ppermute | solution.py:437
  55.3 4.1 %collective-permute-start.8 = (bf16[2,2,128,128]{3,2,1,0:T(8,128)(2,1)S(1)}, bf16[2,2,128,128]{3,2,1,0:T(8,128)(2,1)S(1)}, u32[]{:S(2)}, u32[]{:S(2)}) collective-permute-start(bf16[2,2,128,128]{3,2,1,0:T(8,128)(2,1)S(1)} %get-tuple-element.30), channel_id=1, source_target_pairs={{0,96},{32,0},{64,32},{96,64},{1,97},{33,1},{65,33},{97,65},{2,98}... | collective-permute-start | bytes 393224 | tf_op jit(solution)/shard_map/ppermute | solution.py:429
  59.4 1.3 collective-permute-start.6
  60.6 4.6 %collective-permute-done.8 = bf16[2,2,128,128]{3,2,1,0:T(8,128)(2,1)S(1)} collective-permute-done((bf16[2,2,128,128]{3,2,1,0:T(8,128)(2,1)S(1)}, bf16[2,2,128,128]{3,2,1,0:T(8,128)(2,1)S(1)}, u32[]{:S(2)}, u32[]{:S(2)}) %collective-permute-start.8) | collective-permute-done | bytes 131104 | tf_op jit(solution)/shard_map/ppermute | solution.py:429
  65.3 2.0 collective-permute-done.7
  67.3 1.4 collective-permute-done.6
  70.2 1.4 collective-permute-done.2.b
  71.6 2.5 %sort_heads.1 = bf16[8,4,128,128]{3,2,1,0:T(8,128)(2,1)} custom-call(s32[32]{0:T(128)S(1)} %select_reduce_fusion.source, bf16[8,128,128]{2,1,0:T(8,128)(2,1)S(1)} %get-tuple-element.34.a, bf16[8,128,128]{2,1,0:T(8,128)(2,1)S(1)} %collective-permute-done.2.b, bf16[8,128,128]{2,1,0:T(8,128)(2,1)S(1)} %collective-permute-done.4.c, ...), custom_call_target="tpu_custom_call" | custom-call | bytes 2097152 | tf_op jit(solution)/shard_map/sort_heads/pallas_call | solution.py:241
  74.0 5.2 %all-to-all-start = ((bf16[8,4,128,128]{3,2,1,0:T(8,128)(2,1)}), bf16[8,4,128,128]{3,2,1,0:T(8,128)(2,1)S(1)}, u32[]{:S(2)}, u32[]{:S(2)}) async-start(bf16[8,4,128,128]{3,2,1,0:T(8,128)(2,1)} %sort_heads.1), calls=%async_computation | async-start | bytes 2097152 | tf_op jit(solution)/shard_map/all_to_all | solution.py:456
  81.2 27.8 %all-to-all-done.q_ref = bf16[8,4,128,128]{3,2,1,0:T(8,128)(2,1)S(1)} async-done(((bf16[8,4,128,128]{3,2,1,0:T(8,128)(2,1)}), bf16[8,4,128,128]{3,2,1,0:T(8,128)(2,1)S(1)}, u32[]{:S(2)}, u32[]{:S(2)}) %all-to-all-start) | async-done | bytes 1048608 | tf_op jit(solution)/shard_map/all_to_all | solution.py:456
  109.0 21.7 %all-gather.2.cloned.1.call-done.kv = bf16[16,4,2,2,128,128]{5,4,3,2,1,0:T(8,128)(2,1)} async-done(((bf16[1,4,2,2,128,128]{5,4,3,2,1,0:T(8,128)(2,1)}), bf16[16,4,2,2,128,128]{5,4,3,2,1,0:T(8,128)(2,1)}) %all-gather.2.cloned.1.call-update) | async-done | bytes 8388624 | tf_op jit(solution)/shard_map/all_gather | solution.py:441
  130.7 34.1 %attend.1 = bf16[8,4,128,128]{3,2,1,0:T(8,128)(2,1)} custom-call(s32[8]{0:T(128)} %multiply_add_fusion.blocks, s32[4]{0:T(128)} %convert_reduce_fusion.starts, s32[2]{0:T(128)} %pad_add_fusion.own, bf16[8,4,128,128]{3,2,1,0:T(8,128)(2,1)} %copy-done.4, bf16[16,4,2,2,128,128]{5,4,3,2,1,0:T(8,128)(2,1)} %all-gather.2.cloned.1.call-done.kv), custom_call_target="tpu_custom_call" | custom-call | flops 10000000000 | bytes 10485760 | tf_op jit(solution)/shard_map/attend/pallas_call | solution.py:388
  164.7 26.7 %all_to_all.10.a = bf16[8,4,128,128]{3,2,1,0:T(8,128)(2,1)S(1)} all-to-all(bf16[8,4,128,128]{3,2,1,0:T(8,128)(2,1)} %attend.1), channel_id=1, replica_groups={{0,18,36,54,72,90,108,126},{1,19,37,55,73,91,109,127},{16,2,52,38,88,74..., dimensions={0} | all-to-all | bytes 2097152 | tf_op jit(solution)/shard_map/all_to_all | solution.py:465
  191.5 1.9 unsort_heads.1
  (49 shorter events, 7.0 us)
Async XLA Ops:
  6.5 124.1 %all-gather.2.cloned.1.call-start = ((), (), s32[]{:S(2)}) async-start(), calls=%async_computation.2 | async-start | bytes 8912896 | tf_op jit(solution)/shard_map/all_gather | solution.py:441
  6.5 26.5 %collective-permute-start = (bf16[128,4096]{1,0:T(8,128)(2,1)}, bf16[128,4096]{1,0:T(8,128)(2,1)S(1)}, u32[]{:S(2)}, u32[]{:S(2)}) collective-permute-start(bf16[128,4096]{1,0:T(8,128)(2,1)} %x0.1), channel_id=1, source_target_pairs={{0,18},{1,19},{2,16},{3,17},{4,22},{5,23},{6,20},{7,21},{8,26},{9,... | collective-permute-start | bytes 3145736 | tf_op jit(solution)/shard_map/ppermute | solution.py:417
  9.6 3.0 %collective-permute-start.1 = (bf16[128,4096]{1,0:T(8,128)(2,1)}, bf16[128,4096]{1,0:T(8,128)(2,1)S(1)}, u32[]{:S(2)}, u32[]{:S(2)}) collective-permute-start(bf16[128,4096]{1,0:T(8,128)(2,1)} %x0.1), channel_id=1, source_target_pairs={{0,1},{1,0},{2,3},{3,2},{4,5},{5,4},{6,7},{7,6},{8,9},{9,8},{10,11... | collective-permute-start | bytes 3145736 | tf_op jit(solution)/shard_map/ppermute | solution.py:418
  12.6 0.9 copy-start
  13.6 1.2 copy-start.1
  24.1 0.8 copy-start.2
  33.0 2.7 %collective-permute-start.3 = (bf16[128,4096]{1,0:T(8,128)(2,1)S(1)}, bf16[128,4096]{1,0:T(8,128)(2,1)S(1)}, u32[]{:S(2)}, u32[]{:S(2)}) collective-permute-start(bf16[128,4096]{1,0:T(8,128)(2,1)S(1)} %collective-permute-done.x0), channel_id=1, source_target_pairs={{0,1},{1,0},{2,3},{3,2},{4,5},{5,4},{6,7},{7,6},{8,9},{9,8},{10,11... | collective-permute-start | bytes 3145736 | tf_op jit(solution)/shard_map/ppermute | solution.py:434
  42.2 27.4 %copy-start.6 = (s32[32]{0:T(128)S(1)}, s32[32]{0:T(128)}, u32[]{:S(2)}) copy-start(s32[32]{0:T(128)} %param.11) | copy-start | bytes 388
  42.3 27.6 %copy-start.3 = (bf16[2,8,128,128]{3,2,1,0:T(8,128)(2,1)S(1)}, bf16[2,8,128,128]{3,2,1,0:T(8,128)(2,1)}, u32[]{:S(2)}) copy-start(bf16[2,8,128,128]{3,2,1,0:T(8,128)(2,1)} %copy-done.2) | copy-start | bytes 1572868
  42.3 9.6 %collective-permute-start.4 = (bf16[8,128,128]{2,1,0:T(8,128)(2,1)S(1)}, bf16[8,128,128]{2,1,0:T(8,128)(2,1)S(1)}, u32[]{:S(2)}, u32[]{:S(2)}) collective-permute-start(bf16[8,128,128]{2,1,0:T(8,128)(2,1)S(1)} %get-tuple-element.28), channel_id=1, source_target_pairs={{0,18},{1,19},{2,16},{3,17},{4,22},{5,23},{6,20},{7,21},{8,26},{9,... | collective-permute-start | bytes 786440 | tf_op jit(solution)/shard_map/ppermute | solution.py:436
  45.4 35.0 %copy-start.5 = (s32[16384]{0:T(1024)S(1)}, s32[16384]{0:T(1024)}, u32[]{:S(2)}) copy-start(s32[16384]{0:T(1024)} %param.10) | copy-start | bytes 196612
  52.0 3.1 %collective-permute-start.5 = (bf16[2,2,2,128,128]{4,3,2,0,1:T(8,128)(2,1)S(1)}, bf16[2,2,2,128,128]{4,3,2,0,1:T(8,128)(2,1)S(1)}, u32[]{:S(2)}, u32[]{:S(2)}) collective-permute-start(bf16[2,2,2,128,128]{4,3,2,0,1:T(8,128)(2,1)S(1)} %pad_maximum_fusion), channel_id=1, source_target_pairs={{0,1},{1,0},{2,3},{3,2},{4,5},{5,4},{6,7},{7,6},{8,9},{9,8},{10,11... | collective-permute-start | bytes 786440 | tf_op jit(solution)/shard_map/ppermute | solution.py:424
  52.2 16.6 %collective-permute-start.9 = (bf16[8,128,128]{2,1,0:T(8,128)(2,1)S(1)}, bf16[8,128,128]{2,1,0:T(8,128)(2,1)S(1)}, u32[]{:S(2)}, u32[]{:S(2)}) collective-permute-start(bf16[8,128,128]{2,1,0:T(8,128)(2,1)S(1)} %get-tuple-element.27), channel_id=1, source_target_pairs={{0,19},{1,18},{2,17},{3,16},{4,23},{5,22},{6,21},{7,20},{8,27},{9,... | collective-permute-start | bytes 786440 | tf_op jit(solution)/shard_map/ppermute | solution.py:437
  55.3 10.0 %collective-permute-start.8 = (bf16[2,2,128,128]{3,2,1,0:T(8,128)(2,1)S(1)}, bf16[2,2,128,128]{3,2,1,0:T(8,128)(2,1)S(1)}, u32[]{:S(2)}, u32[]{:S(2)}) collective-permute-start(bf16[2,2,128,128]{3,2,1,0:T(8,128)(2,1)S(1)} %get-tuple-element.30), channel_id=1, source_target_pairs={{0,96},{32,0},{64,32},{96,64},{1,97},{33,1},{65,33},{97,65},{2,98}... | collective-permute-start | bytes 393224 | tf_op jit(solution)/shard_map/ppermute | solution.py:429
  59.4 7.9 %collective-permute-start.7 = (bf16[2,2,128,128]{3,2,1,0:T(8,128)(2,1)S(1)}, bf16[2,2,128,128]{3,2,1,0:T(8,128)(2,1)S(1)}, u32[]{:S(2)}, u32[]{:S(2)}) collective-permute-start(bf16[2,2,128,128]{3,2,1,0:T(8,128)(2,1)S(1)} %get-tuple-element.31), channel_id=1, source_target_pairs={{0,64},{32,96},{64,0},{96,32},{1,65},{33,97},{65,1},{97,33},{2,66}... | collective-permute-start | bytes 393224 | tf_op jit(solution)/shard_map/ppermute | solution.py:429
  59.4 9.3 %collective-permute-start.6 = (bf16[2,2,128,128]{3,2,1,0:T(8,128)(2,1)S(1)}, bf16[2,2,128,128]{3,2,1,0:T(8,128)(2,1)S(1)}, u32[]{:S(2)}, u32[]{:S(2)}) collective-permute-start(bf16[2,2,128,128]{3,2,1,0:T(8,128)(2,1)S(1)} %get-tuple-element.32), channel_id=1, source_target_pairs={{0,32},{32,64},{64,96},{96,0},{1,33},{33,65},{65,97},{97,1},{2,34}... | collective-permute-start | bytes 393224 | tf_op jit(solution)/shard_map/ppermute | solution.py:429
  69.9 1.6 collective-permute-start.2
  74.0 34.9 %all-to-all-start = ((bf16[8,4,128,128]{3,2,1,0:T(8,128)(2,1)}), bf16[8,4,128,128]{3,2,1,0:T(8,128)(2,1)S(1)}, u32[]{:S(2)}, u32[]{:S(2)}) async-start(bf16[8,4,128,128]{3,2,1,0:T(8,128)(2,1)} %sort_heads.1), calls=%async_computation | async-start | bytes 2097152 | tf_op jit(solution)/shard_map/all_to_all | solution.py:456
  109.0 21.7 %copy-start.4 = (bf16[8,4,128,128]{3,2,1,0:T(8,128)(2,1)}, bf16[8,4,128,128]{3,2,1,0:T(8,128)(2,1)S(1)}, u32[]{:S(2)}) copy-start(bf16[8,4,128,128]{3,2,1,0:T(8,128)(2,1)S(1)} %all-to-all-done.q_ref) | copy-start | bytes 3145732
Sparse Core Ops, SparseCore 0:
  69.8 60.8 all-gather.1

commit v4 on v3

--- a/solution.py
+++ b/solution.py
@@ -267,16 +267,19 @@
     )(slots, a)
 
 
-def attend_kernel(blocks, starts, own, q_ref, kv, out, pairs, sems, top, total, acc, floor):
+def attend_kernel(blocks, starts, own, q_ref, kv0, kv1, out, pairs, sems, top, total, acc, floor):
     yh = own[0]
 
-    def copy_of(z):
-        return pltpu.make_async_copy(
-            kv.at[:, pl.ds((own[1] - z + NZ) % NZ, 1)], pairs.at[:, pl.ds(z, 1)], sems.at[z]
-        )
+    def copies_of(z):
+        row = (own[1] - z + NZ) % NZ
+        return [
+            pltpu.make_async_copy(src.at[:, pl.ds(row, 1)], pairs.at[stage, :, pl.ds(z, 1)], sems.at[2 * z + stage])
+            for stage, src in enumerate((kv0, kv1))
+        ]
 
     for z in range(NZ):
-        copy_of(z).start()
+        for copy in copies_of(z):
+            copy.start()
 
     def gathered(begin_block, width, kind):
         parts = []
@@ -285,7 +288,7 @@
             low = (key_block // (NC * NYH * NX)) % NYL
             stage = ((key_block // NC) % NYH) ^ yh
             source = (((key_block // (NC * NYH)) % NX) * NYL + (low ^ stage)) * NC + key_block % NC
-            parts.append(pairs[source, key_block // (NC * NYH * NX * NYL), stage, kind])
+            parts.append(pairs[stage, source, key_block // (NC * NYH * NX * NYL), kind])
         return jnp.concatenate(parts, axis=0)
 
     def one_tile(tile):
@@ -375,7 +378,8 @@
         out[tile] = (acc[...] / jnp.sum(total[...], axis=1, keepdims=True)).astype(BF).reshape(4, BLK, DH)
 
     def pair(z, carry):
-        copy_of(z).wait()
+        for copy in copies_of(z):
+            copy.wait()
         one_tile(2 * z)
         one_tile(2 * z + 1)
         return carry
@@ -383,7 +387,7 @@
     lax.fori_loop(0, NZ, pair, 0)
 
 
-def attend(blocks, starts, own, q, kv):
+def attend(blocks, starts, own, q, kv0, kv1):
     rows = 4 * BLK
     return pl.pallas_call(
         attend_kernel,
@@ -391,12 +395,13 @@
         + [
             pl.BlockSpec(memory_space=pltpu.VMEM),
             pl.BlockSpec(memory_space=pl.ANY),
+            pl.BlockSpec(memory_space=pl.ANY),
         ],
         out_specs=pl.BlockSpec(memory_space=pltpu.VMEM),
         out_shape=jax.ShapeDtypeStruct((8, 4, BLK, DH), BF),
         scratch_shapes=[
-            pltpu.VMEM((NX * NYL * NC, NZ, 2, 2, BLK, DH), BF),
-            pltpu.SemaphoreType.DMA((NZ,)),
+            pltpu.VMEM((2, NX * NYL * NC, NZ, 2, BLK, DH), BF),
+            pltpu.SemaphoreType.DMA((2 * NZ,)),
             pltpu.VMEM((rows, DH), F32),
             pltpu.VMEM((rows, DH), F32),
             pltpu.VMEM((rows, DH), F32),
@@ -405,7 +410,7 @@
         compiler_params=pltpu.CompilerParams(vmem_limit_bytes=60 * 2**20),
         cost_estimate=pl.CostEstimate(flops=10**10, bytes_accessed=10 * 2**20, transcendentals=10**7),
         name="attend",
-    )(blocks, starts, own, q, kv)
+    )(blocks, starts, own, q, kv0, kv1)
 
 
 def per_device(tokens, w, down, up, document_index, query_to_key_head):
@@ -420,25 +425,30 @@
     near_cos, near_sin = rope_tables(jnp.stack([block, block + other]))
     far_cos, far_sin = rope_tables(jnp.stack([far_block, far_block + other]))
 
-    def split_kv(near, far):
-        mine, theirs = jnp.stack([near[0], far[0]], 1), lax.ppermute(jnp.stack([near[1], far[1]], 1), "c", SWAP)
+    def split_kv(part, beside=None):
+        mine, theirs = part[0], lax.ppermute(part[1], "c", SWAP)
         heads = jnp.where(c == 0, jnp.concatenate([mine, theirs], 0), jnp.concatenate([theirs, mine], 0))
         rows = []
         for k in range(NZ):
             head = lax.dynamic_index_in_dim(heads, (z + k) % NZ, 0, keepdims=False)
             rows.append(lax.ppermute(head, "z", [(i, (i + k) % NZ) for i in range(NZ)]) if k else head)
+        if beside is not None:
+            rows, _ = lax.optimization_barrier((rows, beside))
         return jnp.stack(rows)[None]
 
     q_near, kv_near = project_both(tokens, near_pair, w, down, up, near_cos, near_sin)
     far, q_near, kv_near = lax.optimization_barrier((far, q_near, kv_near))
     far_pair = lax.ppermute(far, "c", SWAP)
     q_far, mid_far = project(False, far, far_pair, w, down, up, far_cos, far_sin)
+    rows_near = split_kv(kv_near, mid_far)
+    kv0 = lax.all_gather(rows_near, ("x", "yl", "c"), axis=0, tiled=True)
+    mid_far, _ = lax.optimization_barrier((mid_far, rows_near))
     home_c = lax.ppermute(q_far[0], ALL, CROSS)
     home_d = lax.ppermute(q_far[1], ALL, CROSS_OTHER)
     kv_far = project(True, far, far_pair, w, mid_far, up, far_cos, far_sin)
     kv_far, home_c = lax.optimization_barrier((kv_far, home_c))
-    rows, home_d = lax.optimization_barrier((split_kv(kv_near, kv_far), home_d))
-    kv = lax.all_gather(rows, ("x", "yl", "c"), axis=0, tiled=True)
+    rows_far, home_d = lax.optimization_barrier((split_kv(kv_far), home_d))
+    kv1 = lax.all_gather(rows_far, ("x", "yl", "c"), axis=0, tiled=True)
 
     parts = (
         q_near[0],
@@ -461,7 +471,7 @@
     starts = jnp.sum(
         (document_index[None, :] < jnp.arange(DOCS, dtype=jnp.int32)[:, None]).astype(jnp.int32), axis=1
     )
-    context = attend(blocks, starts, jnp.stack([yh, z]).astype(jnp.int32), q, kv)
+    context = attend(blocks, starts, jnp.stack([yh, z]).astype(jnp.int32), q, kv0, kv1)
     home = lax.all_to_all(context, ALL, split_axis=0, concat_axis=0, tiled=True, axis_index_groups=GROUPS)
     return unsort_heads(slots, home)
 

time: 204 us -> 200 us (0.980); the launches traced: 200 us -> 202 us
  waiting for transfers between devices: 72.6 us -> 59.9 us
  starting transfers between devices: 19.9 us -> 27.1 us
  other arithmetic: 4.01 us -> 8.84 us
  local copies, waits for them, and re-layouts: 5.54 us -> 9.72 us
  Pallas kernels: 57.7 us -> 54.3 us
    all_to_all x1, waiting for transfers between devices: 27.8 us -> 17.6 us  [per_device(): lax.all_to_all(sorted_q, ALL, split_axis=0, concat_axis=0, tiled=True, ax...]
    all_gather x1 -> x2, waiting for transfers between devices: 21.7 us -> 27.7 us  [the longest x1 27.7 us: per_device(): kv1 = lax.all_gather(rows_far, ('x', 'yl', 'c'), axis=0, tiled=True)]
    ppermute x3 -> x6, starting transfers between devices: 5.37 us -> 10.4 us  [split_kv(): lax.ppermute(head, 'z', [(i, (i + k) % NZ) for i in range(NZ)])]
    ppermute x3 -> x6, waiting for transfers between devices: 8.03 us -> 3.49 us  [split_kv(): lax.ppermute(head, 'z', [(i, (i + k) % NZ) for i in range(NZ)])]
    pallas_call x1, Pallas kernels: 34.1 us -> 30.5 us  [attend(): pl.pallas_call(attend_kernel, in_specs=[pl.BlockSpec(memory_space=pltpu.S...]
    unnamed x15 -> x23, local copies, waits for them, and re-layouts: 4.48 us -> 7.1 us
    ppermute x1, waiting for transfers between devices: 2.44 us -> 0.01 us  [per_device(): far_pair = lax.ppermute(far, 'c', SWAP)]
  transfers between devices with their start and end apart: 12 -> 17, of which waited for: 9 -> 8; matrix products, arithmetic and copies ran while one was open for 3% -> 6% of each run, Pallas kernels for 8% -> 11%
where the time goes in v4:
time: 200 us; the launch traced here: 202 us
  waiting for transfers between devices  59.9 us (30%)
  Pallas kernels  54.3 us (27%)
  blocking collectives  28.3 us (14%)
  starting transfers between devices  27.1 us (14%)
  between operations  13.6 us (7%)
  local copies, waits for them, and re-layouts  9.72 us (5%)
  other arithmetic  8.84 us (4%)
    pallas_call x1, Pallas kernels, attend(): pl.pallas_call(attend_kernel, in_specs=[pl.BlockSpec(memory_space=pltpu.S...  30.5 us
    all_to_all x1, blocking collectives, per_device(): lax.all_to_all(context, ALL, split_axis=0, concat_axis=0, tiled=True, axi...  28.3 us
    all_gather x1, waiting for transfers between devices, per_device(): kv1 = lax.all_gather(rows_far, ('x', 'yl', 'c'), axis=0, tiled=True)  27.7 us
    all_to_all x1, waiting for transfers between devices, per_device(): lax.all_to_all(sorted_q, ALL, split_axis=0, concat_axis=0, tiled=True, ax...  17.6 us
    ppermute x6, starting transfers between devices, split_kv(): lax.ppermute(head, 'z', [(i, (i + k) % NZ) for i in range(NZ)])  10.4 us
    pallas_call x2, Pallas kernels, project(): pl.pallas_call(functools.partial(kv_kernel if for_keys else q_kernel, mak...  10 us
    pallas_call x1, Pallas kernels, project_both(): pl.pallas_call(both_kernel, grid=(6,), in_specs=[whole((BLK, width)), who...  9.33 us
    ppermute x1, waiting for transfers between devices, per_device(): far = lax.ppermute(tokens, ALL, CROSS)  8.2 us
  transfers between devices with their start and end apart: 17, of which 8 were waited for; matrix products, arithmetic and copies ran while one was open for 6% of the time, Pallas kernels for 11%

profile of v4, /device:TPU:0, one launch (start us, length us, event | category | flops | bytes accessed | tf_op | source)
XLA Modules:
  0.0 201.8 jit_solution(10200302795254298561)
XLA Ops:
  6.5 3.1 %collective-permute-start = (bf16[128,4096]{1,0:T(8,128)(2,1)}, bf16[128,4096]{1,0:T(8,128)(2,1)S(1)}, u32[]{:S(2)}, u32[]{:S(2)}) collective-permute-start(bf16[128,4096]{1,0:T(8,128)(2,1)} %x0.1), channel_id=1, source_target_pairs={{0,18},{1,19},{2,16},{3,17},{4,22},{5,23},{6,20},{7,21},{8,26},{9,... | collective-permute-start | bytes 3145736 | tf_op jit(solution)/shard_map/ppermute | solution.py:422
  9.8 1.5 copy.11.low
  11.4 1.6 fusion.1
  14.1 1.2 copy-done.4
  15.3 9.3 %project_both.1 = (bf16[2,8,128,128]{3,2,1,0:T(8,128)(2,1)S(1)}, bf16[2,2,2,128,128]{4,3,2,1,0:T(8,128)(2,1)S(1)}) custom-call(bf16[128,4096]{1,0:T(8,128)(2,1)S(1)} %copy-done.4, bf16[128,4096]{1,0:T(8,128)(2,1)S(1)} %collective-permute-done.1.x1, bf16[4096,1536]{1,0:T(8,128)(2,1)} %w.5, bf16[4096,64]{1,0:T(8,128)(2,1)S(1)} %copy.11.low, ...), custom_call_target="tpu_custom_call" | custom-call | flops 3221225472 | bytes 12582912 | tf_op jit(solution)/shard_map/project_both/pallas_call | solution.py:157
  25.5 8.2 %collective-permute-done.x0 = bf16[128,4096]{1,0:T(8,128)(2,1)S(1)} collective-permute-done((bf16[128,4096]{1,0:T(8,128)(2,1)}, bf16[128,4096]{1,0:T(8,128)(2,1)S(1)}, u32[]{:S(2)}, u32[]{:S(2)}) %collective-permute-start) | collective-permute-done | bytes 1048608 | tf_op jit(solution)/shard_map/ppermute | solution.py:422
  38.0 2.0 collective-permute-start.5
  40.0 3.6 %collective-permute-start.6 = (bf16[2,128,128]{2,1,0:T(8,128)(2,1)S(1)}, bf16[2,128,128]{2,1,0:T(8,128)(2,1)S(1)}, u32[]{:S(2)}, u32[]{:S(2)}) collective-permute-start(bf16[2,128,128]{2,1,0:T(8,128)(2,1)S(1)} %get-tuple-element.42), channel_id=1, source_target_pairs={{0,64},{32,96},{64,0},{96,32},{1,65},{33,97},{65,1},{97,33},{2,66}... | collective-permute-start | bytes 196616 | tf_op jit(solution)/shard_map/ppermute | solution.py:434
  45.5 6.6 %project_q.1 = (bf16[2,8,128,128]{3,2,1,0:T(8,128)(2,1)S(1)}, bf16[256,64]{1,0:T(8,128)(2,1)S(1)}) custom-call(bf16[128,4096]{1,0:T(8,128)(2,1)S(1)} %collective-permute-done.x0, bf16[128,4096]{1,0:T(8,128)(2,1)S(1)} %collective-permute-done.3.x1, bf16[4096,1536]{1,0:T(8,128)(2,1)} %w.5, bf16[4096,64]{1,0:T(8,128)(2,1)S(1)} %copy.11.low, ...), custom_call_target="tpu_custom_call" | custom-call | flops 2147483648 | bytes 8388608 | tf_op jit(solution)/shard_map/project_q/pallas_call | solution.py:204
  53.8 1.8 slice_bitcast_fusion
  55.6 3.0 %collective-permute-start.8 = (bf16[8,128,128]{2,1,0:T(8,128)(2,1)S(1)}, bf16[8,128,128]{2,1,0:T(8,128)(2,1)S(1)}, u32[]{:S(2)}, u32[]{:S(2)}) collective-permute-start(bf16[8,128,128]{2,1,0:T(8,128)(2,1)S(1)} %get-tuple-element.38), channel_id=1, source_target_pairs={{0,18},{1,19},{2,16},{3,17},{4,22},{5,23},{6,20},{7,21},{8,26},{9,... | collective-permute-start | bytes 786440 | tf_op jit(solution)/shard_map/ppermute | solution.py:446
  59.4 3.5 %project_kv.1 = bf16[2,2,2,128,128]{4,3,2,1,0:T(8,128)(2,1)S(1)} custom-call(bf16[128,4096]{1,0:T(8,128)(2,1)S(1)} %collective-permute-done.x0, bf16[128,4096]{1,0:T(8,128)(2,1)S(1)} %collective-permute-done.3.x1, bf16[4096,1536]{1,0:T(8,128)(2,1)} %w.5, bf16[256,64]{1,0:T(8,128)(2,1)S(1)} %get-tuple-element.31.low, bf16[64,1536]{1,0:T(8,128)(2,1)S(1)} %copy-done.1, ...), custom_call_target="tpu_custom_call" | custom-call | flops 1073741824 | bytes 4194304 | tf_op jit(solution)/shard_map/project_kv/pallas_call | solution.py:204
  62.9 1.4 collective-permute-done.8.c
  64.4 3.1 %collective-permute-start.13 = (bf16[8,128,128]{2,1,0:T(8,128)(2,1)}, bf16[8,128,128]{2,1,0:T(8,128)(2,1)S(1)}, u32[]{:S(2)}, u32[]{:S(2)}) collective-permute-start(bf16[8,128,128]{2,1,0:T(8,128)(2,1)} %get-tuple-element.37), channel_id=1, source_target_pairs={{0,19},{1,18},{2,17},{3,16},{4,23},{5,22},{6,21},{7,20},{8,27},{9,... | collective-permute-start | bytes 786440 | tf_op jit(solution)/shard_map/ppermute | solution.py:447
  69.4 2.0 %collective-permute-start.12 = (bf16[2,128,128]{2,1,0:T(8,128)(2,1)S(1)}, bf16[2,128,128]{2,1,0:T(8,128)(2,1)S(1)}, u32[]{:S(2)}, u32[]{:S(2)}) collective-permute-start(bf16[2,128,128]{2,1,0:T(8,128)(2,1)S(1)} %get-tuple-element.48), channel_id=1, source_target_pairs={{0,96},{32,0},{64,32},{96,64},{1,97},{33,1},{65,33},{97,65},{2,98}... | collective-permute-start | bytes 196616 | tf_op jit(solution)/shard_map/ppermute | solution.py:434
  71.4 3.1 %collective-permute-done.10 = bf16[2,128,128]{2,1,0:T(8,128)(2,1)S(1)} collective-permute-done((bf16[2,128,128]{2,1,0:T(8,128)(2,1)S(1)}, bf16[2,128,128]{2,1,0:T(8,128)(2,1)S(1)}, u32[]{:S(2)}, u32[]{:S(2)}) %collective-permute-start.10) | collective-permute-done | bytes 65568 | tf_op jit(solution)/shard_map/ppermute | solution.py:434
  76.2 1.4 collective-permute-done.2.b
  77.5 2.5 %sort_heads.1 = bf16[8,4,128,128]{3,2,1,0:T(8,128)(2,1)} custom-call(s32[32]{0:T(128)S(1)} %select_reduce_fusion.source, bf16[8,128,128]{2,1,0:T(8,128)(2,1)S(1)} %get-tuple-element.40.a, bf16[8,128,128]{2,1,0:T(8,128)(2,1)S(1)} %collective-permute-done.2.b, bf16[8,128,128]{2,1,0:T(8,128)(2,1)S(1)} %collective-permute-done.8.c, ...), custom_call_target="tpu_custom_call" | custom-call | bytes 2097152 | tf_op jit(solution)/shard_map/sort_heads/pallas_call | solution.py:241
  80.0 6.9 %all-to-all-start = ((bf16[8,4,128,128]{3,2,1,0:T(8,128)(2,1)}), bf16[8,4,128,128]{3,2,1,0:T(8,128)(2,1)S(1)}, u32[]{:S(2)}, u32[]{:S(2)}) async-start(bf16[8,4,128,128]{3,2,1,0:T(8,128)(2,1)} %sort_heads.1), calls=%async_computation | async-start | bytes 2097152 | tf_op jit(solution)/shard_map/all_to_all | solution.py:466
  88.9 17.6 %all-to-all-done.q_ref = bf16[8,4,128,128]{3,2,1,0:T(8,128)(2,1)S(1)} async-done(((bf16[8,4,128,128]{3,2,1,0:T(8,128)(2,1)}), bf16[8,4,128,128]{3,2,1,0:T(8,128)(2,1)S(1)}, u32[]{:S(2)}, u32[]{:S(2)}) %all-to-all-start) | async-done | bytes 1048608 | tf_op jit(solution)/shard_map/all_to_all | solution.py:466
  106.5 27.7 %all-gather.4.cloned.1.call-done.kv1 = bf16[16,4,2,128,128]{4,3,2,1,0:T(8,128)(2,1)} async-done(((bf16[1,4,2,128,128]{4,3,2,1,0:T(8,128)(2,1)}), bf16[16,4,2,128,128]{4,3,2,1,0:T(8,128)(2,1)}) %all-gather.4.cloned.1.call-update) | async-done | bytes 4194320 | tf_op jit(solution)/shard_map/all_gather | solution.py:451
  134.2 30.5 %attend.1 = bf16[8,4,128,128]{3,2,1,0:T(8,128)(2,1)} custom-call(s32[8]{0:T(128)} %multiply_add_fusion.blocks, s32[4]{0:T(128)} %convert_reduce_fusion.starts, s32[2]{0:T(128)} %pad_add_fusion.own, bf16[8,4,128,128]{3,2,1,0:T(8,128)(2,1)} %copy-done.8, bf16[16,4,2,128,128]{4,3,2,1,0:T(8,128)(2,1)} %bitcast.57, ...), custom_call_target="tpu_custom_call" | custom-call | flops 10000000000 | bytes 10485760 | tf_op jit(solution)/shard_map/attend/pallas_call | solution.py:392
  164.7 28.3 %all_to_all.10.a = bf16[8,4,128,128]{3,2,1,0:T(8,128)(2,1)S(1)} all-to-all(bf16[8,4,128,128]{3,2,1,0:T(8,128)(2,1)} %attend.1), channel_id=1, replica_groups={{0,18,36,54,72,90,108,126},{1,19,37,55,73,91,109,127},{16,2,52,38,88,74..., dimensions={0} | all-to-all | bytes 2097152 | tf_op jit(solution)/shard_map/all_to_all | solution.py:475
  193.0 1.9 unsort_heads.1
  (69 shorter events, 16.6 us)
Async XLA Ops:
  6.5 100.0 %all-gather.6.cloned.1.call-start = ((), (), s32[]{:S(2)}) async-start(), calls=%async_computation.3 | async-start | bytes 4456448 | tf_op jit(solution)/shard_map/all_gather | solution.py:444
  6.5 6.6 %collective-permute-start.1 = (bf16[128,4096]{1,0:T(8,128)(2,1)}, bf16[128,4096]{1,0:T(8,128)(2,1)S(1)}, u32[]{:S(2)}, u32[]{:S(2)}) collective-permute-start(bf16[128,4096]{1,0:T(8,128)(2,1)} %x0.1), channel_id=1, source_target_pairs={{0,1},{1,0},{2,3},{3,2},{4,5},{5,4},{6,7},{7,6},{8,9},{9,8},{10,11... | collective-permute-start | bytes 3145736 | tf_op jit(solution)/shard_map/ppermute | solution.py:423
  6.5 27.1 %collective-permute-start = (bf16[128,4096]{1,0:T(8,128)(2,1)}, bf16[128,4096]{1,0:T(8,128)(2,1)S(1)}, u32[]{:S(2)}, u32[]{:S(2)}) collective-permute-start(bf16[128,4096]{1,0:T(8,128)(2,1)} %x0.1), channel_id=1, source_target_pairs={{0,18},{1,19},{2,16},{3,17},{4,22},{5,23},{6,20},{7,21},{8,26},{9,... | collective-permute-start | bytes 3145736 | tf_op jit(solution)/shard_map/ppermute | solution.py:422
  13.2 0.9 copy-start
  14.1 1.2 copy-start.4
  15.3 29.3 %copy-start.1 = (bf16[64,1536]{1,0:T(8,128)(2,1)S(1)}, bf16[64,1536]{1,0:T(8,128)(2,1)}, u32[]{:S(2)}) copy-start(bf16[64,1536]{1,0:T(8,128)(2,1)} %up.5) | copy-start | bytes 589828
  33.7 11.0 %collective-permute-start.3 = (bf16[128,4096]{1,0:T(8,128)(2,1)S(1)}, bf16[128,4096]{1,0:T(8,128)(2,1)S(1)}, u32[]{:S(2)}, u32[]{:S(2)}) collective-permute-start(bf16[128,4096]{1,0:T(8,128)(2,1)S(1)} %collective-permute-done.x0), channel_id=1, source_target_pairs={{0,1},{1,0},{2,3},{3,2},{4,5},{5,4},{6,7},{7,6},{8,9},{9,8},{10,11... | collective-permute-start | bytes 3145736 | tf_op jit(solution)/shard_map/ppermute | solution.py:441
  34.4 2.5 %collective-permute-start.4 = (bf16[2,2,128,128]{3,2,1,0:T(8,128)(2,1)}, bf16[2,2,128,128]{3,2,1,0:T(8,128)(2,1)}, u32[]{:S(2)}, u32[]{:S(2)}) collective-permute-start(bf16[2,2,128,128]{3,2,1,0:T(8,128)(2,1)} %get-tuple-element.46), channel_id=1, source_target_pairs={{0,1},{1,0},{2,3},{3,2},{4,5},{5,4},{6,7},{7,6},{8,9},{9,8},{10,11... | collective-permute-start | bytes 393224 | tf_op jit(solution)/shard_map/ppermute | solution.py:429
  38.0 14.9 %collective-permute-start.5 = (bf16[2,128,128]{2,1,0:T(8,128)(2,1)S(1)}, bf16[2,128,128]{2,1,0:T(8,128)(2,1)S(1)}, u32[]{:S(2)}, u32[]{:S(2)}) collective-permute-start(bf16[2,128,128]{2,1,0:T(8,128)(2,1)S(1)} %get-tuple-element.43), channel_id=1, source_target_pairs={{0,32},{32,64},{64,96},{96,0},{1,33},{33,65},{65,97},{97,1},{2,34}... | collective-permute-start | bytes 196616 | tf_op jit(solution)/shard_map/ppermute | solution.py:434
  40.0 12.9 %collective-permute-start.6 = (bf16[2,128,128]{2,1,0:T(8,128)(2,1)S(1)}, bf16[2,128,128]{2,1,0:T(8,128)(2,1)S(1)}, u32[]{:S(2)}, u32[]{:S(2)}) collective-permute-start(bf16[2,128,128]{2,1,0:T(8,128)(2,1)S(1)} %get-tuple-element.42), channel_id=1, source_target_pairs={{0,64},{32,96},{64,0},{96,32},{1,65},{33,97},{65,1},{97,33},{2,66}... | collective-permute-start | bytes 196616 | tf_op jit(solution)/shard_map/ppermute | solution.py:434
  43.6 9.3 %collective-permute-start.7 = (bf16[2,128,128]{2,1,0:T(8,128)(2,1)S(1)}, bf16[2,128,128]{2,1,0:T(8,128)(2,1)S(1)}, u32[]{:S(2)}, u32[]{:S(2)}) collective-permute-start(bf16[2,128,128]{2,1,0:T(8,128)(2,1)S(1)} %get-tuple-element.41), channel_id=1, source_target_pairs={{0,96},{32,0},{64,32},{96,64},{1,97},{33,1},{65,33},{97,65},{2,98}... | collective-permute-start | bytes 196616 | tf_op jit(solution)/shard_map/ppermute | solution.py:434
  53.7 80.5 %all-gather.4.cloned.1.call-start = ((), (), s32[]{:S(2)}) async-start(), calls=%async_computation.2 | async-start | bytes 4456448 | tf_op jit(solution)/shard_map/all_gather | solution.py:451
  55.6 8.7 %collective-permute-start.8 = (bf16[8,128,128]{2,1,0:T(8,128)(2,1)S(1)}, bf16[8,128,128]{2,1,0:T(8,128)(2,1)S(1)}, u32[]{:S(2)}, u32[]{:S(2)}) collective-permute-start(bf16[8,128,128]{2,1,0:T(8,128)(2,1)S(1)} %get-tuple-element.38), channel_id=1, source_target_pairs={{0,18},{1,19},{2,16},{3,17},{4,22},{5,23},{6,20},{7,21},{8,26},{9,... | collective-permute-start | bytes 786440 | tf_op jit(solution)/shard_map/ppermute | solution.py:446
  59.4 16.3 %copy-start.10 = (s32[32]{0:T(128)S(1)}, s32[32]{0:T(128)}, u32[]{:S(2)}) copy-start(s32[32]{0:T(128)} %param.11) | copy-start | bytes 388
  59.4 16.5 %copy-start.6 = (bf16[2,8,128,128]{3,2,1,0:T(8,128)(2,1)S(1)}, bf16[2,8,128,128]{3,2,1,0:T(8,128)(2,1)}, u32[]{:S(2)}) copy-start(bf16[2,8,128,128]{3,2,1,0:T(8,128)(2,1)} %copy-done.5) | copy-start | bytes 1572868
  62.9 25.2 %copy-start.9 = (s32[16384]{0:T(1024)S(1)}, s32[16384]{0:T(1024)}, u32[]{:S(2)}) copy-start(s32[16384]{0:T(1024)} %param.10) | copy-start | bytes 196612
  64.3 3.2 %collective-permute-start.9 = (bf16[2,2,128,128]{3,2,1,0:T(8,128)(2,1)S(1)}, bf16[2,2,128,128]{3,2,1,0:T(8,128)(2,1)S(1)}, u32[]{:S(2)}, u32[]{:S(2)}) collective-permute-start(bf16[2,2,128,128]{3,2,1,0:T(8,128)(2,1)S(1)} %get-tuple-element.52), channel_id=1, source_target_pairs={{0,1},{1,0},{2,3},{3,2},{4,5},{5,4},{6,7},{7,6},{8,9},{9,8},{10,11... | collective-permute-start | bytes 393224 | tf_op jit(solution)/shard_map/ppermute | solution.py:429
  64.4 11.2 %collective-permute-start.13 = (bf16[8,128,128]{2,1,0:T(8,128)(2,1)}, bf16[8,128,128]{2,1,0:T(8,128)(2,1)S(1)}, u32[]{:S(2)}, u32[]{:S(2)}) collective-permute-start(bf16[8,128,128]{2,1,0:T(8,128)(2,1)} %get-tuple-element.37), channel_id=1, source_target_pairs={{0,19},{1,18},{2,17},{3,16},{4,23},{5,22},{6,21},{7,20},{8,27},{9,... | collective-permute-start | bytes 786440 | tf_op jit(solution)/shard_map/ppermute | solution.py:447
  67.5 7.0 %collective-permute-start.10 = (bf16[2,128,128]{2,1,0:T(8,128)(2,1)S(1)}, bf16[2,128,128]{2,1,0:T(8,128)(2,1)S(1)}, u32[]{:S(2)}, u32[]{:S(2)}) collective-permute-start(bf16[2,128,128]{2,1,0:T(8,128)(2,1)S(1)} %get-tuple-element.50), channel_id=1, source_target_pairs={{0,32},{32,64},{64,96},{96,0},{1,33},{33,65},{65,97},{97,1},{2,34}... | collective-permute-start | bytes 196616 | tf_op jit(solution)/shard_map/ppermute | solution.py:434
  68.6 5.9 %collective-permute-start.11 = (bf16[2,128,128]{2,1,0:T(8,128)(2,1)S(1)}, bf16[2,128,128]{2,1,0:T(8,128)(2,1)S(1)}, u32[]{:S(2)}, u32[]{:S(2)}) collective-permute-start(bf16[2,128,128]{2,1,0:T(8,128)(2,1)S(1)} %get-tuple-element.49), channel_id=1, source_target_pairs={{0,64},{32,96},{64,0},{96,32},{1,65},{33,97},{65,1},{97,33},{2,66}... | collective-permute-start | bytes 196616 | tf_op jit(solution)/shard_map/ppermute | solution.py:434
  69.4 5.5 %collective-permute-start.12 = (bf16[2,128,128]{2,1,0:T(8,128)(2,1)S(1)}, bf16[2,128,128]{2,1,0:T(8,128)(2,1)S(1)}, u32[]{:S(2)}, u32[]{:S(2)}) collective-permute-start(bf16[2,128,128]{2,1,0:T(8,128)(2,1)S(1)} %get-tuple-element.48), channel_id=1, source_target_pairs={{0,96},{32,0},{64,32},{96,64},{1,97},{33,1},{65,33},{97,65},{2,98}... | collective-permute-start | bytes 196616 | tf_op jit(solution)/shard_map/ppermute | solution.py:434
  75.9 1.6 collective-permute-start.2
  80.0 26.5 %all-to-all-start = ((bf16[8,4,128,128]{3,2,1,0:T(8,128)(2,1)}), bf16[8,4,128,128]{3,2,1,0:T(8,128)(2,1)S(1)}, u32[]{:S(2)}, u32[]{:S(2)}) async-start(bf16[8,4,128,128]{3,2,1,0:T(8,128)(2,1)} %sort_heads.1), calls=%async_computation | async-start | bytes 2097152 | tf_op jit(solution)/shard_map/all_to_all | solution.py:466
  106.5 27.7 %copy-start.8 = (bf16[8,4,128,128]{3,2,1,0:T(8,128)(2,1)}, bf16[8,4,128,128]{3,2,1,0:T(8,128)(2,1)S(1)}, u32[]{:S(2)}) copy-start(bf16[8,4,128,128]{3,2,1,0:T(8,128)(2,1)S(1)} %all-to-all-done.q_ref) | copy-start | bytes 3145732
  (4 other events, 3.4 us)
Sparse Core Ops, SparseCore 0:
  53.8 37.5 all-gather.5
  93.2 40.9 all-gather.3
